TPU v7x, 256 devices: a whole 4x4x8 slice. The times are simulated.
256 devices in a mesh: band: 16 (over z, y_lo), fft: 16 (over y_hi, x, core).
Axes of the slice: x: 4, y: 4 (y_hi: 2, y_lo: 2; y = y_hi * 2 + y_lo), z: 8, core: 2. Of those that a mesh axis runs over, the one named last changes fastest.
Arguments:
- wavefunctions: bfloat16 [16, 176, 30976], P('band', 'fft'), may hold values from -6 to 6
- band_occ: int32 [16], P('band'), may hold values from 0 to 2
Outputs:
- exchange_term: float32 [16, 176, 30976], P('band', 'fft')
All inputs are finite; a program needn't handle non-finite values.
Results may differ from a plain program's by a relative error of at most 0.0003.
Values may be sent and summed in bfloat16 or wider, within the bound.
No kernel may reach another device: no remote copies, remote signals or barrier semaphores. Data moves between devices by JAX's collectives and lax.ppermute only.
A program may use at most 64 MiB of HBM per device.

v0:
```python
import functools

import jax
import jax.numpy as jnp
import ml_dtypes
import numpy as np
from jax import lax
from jax.experimental import pallas as pl
from jax.experimental.pallas import tpu as pltpu
from jax.sharding import PartitionSpec as P

NG = 176
FFT = 16
SLAB = 11
LANES = 128
STEPS = 11
GROUPS = 22
ROWS = 256
OCC_ROW = 248
CELLS = 121
BLOCK = 128
EXP_ROW = 121
PARTS = 3
F32 = jnp.float32
BF16 = jnp.bfloat16

WINDOWS = []
for _j in range(8):
    _first, _offset = divmod(NG * _j, LANES)
    WINDOWS.append((_first, _offset, -(-(_offset + NG) // LANES)))

LOW = list(range(8)) + list(range(168, 176))
KZ_FIRST = list(range(128))
KZ_REST = list(range(128, 176)) + LOW


def split_table(table):
    high = table.astype(ml_dtypes.bfloat16)
    low = (table - high.astype(np.float64)).astype(ml_dtypes.bfloat16)
    return np.stack([high, low])


@functools.cache
def tables():
    index = np.arange(NG)
    phase = (index[:, None] * index[None, :] % NG) * (2.0 * np.pi / NG)
    cas = np.cos(phase) + np.sin(phase)
    lanes = np.array(KZ_FIRST + KZ_REST + KZ_REST)
    z_forward = np.zeros((400, 256))
    z_forward[112 : 112 + NG] = cas[:, lanes]
    y_forward = np.zeros((FFT, 16, 256))
    planes = np.zeros((FFT, 16, 256))
    for block in range(FFT):
        own = block * SLAB + np.arange(SLAB)
        planes[block, :SLAB, :NG] = cas[own]
        for j in range(8):
            rows = 8 * np.arange(GROUPS) + j
            y_forward[block, :SLAB, 24 * j : 24 * j + GROUPS] = cas[own][:, rows]
    y_forward = y_forward.reshape(256, 256)
    x_back = planes.reshape(256, 256)
    x_forward = x_back.T[:NG]
    y_back = y_forward.T[:192]
    z_back = np.zeros((8, 320, 384))
    for j, (_, offset, _) in enumerate(WINDOWS):
        z_back[j, :128, offset : offset + NG] = cas[KZ_FIRST]
        z_back[j, 192:256, offset : offset + NG] = cas[KZ_REST]
    return {
        "zf": split_table(z_forward),
        "yf": split_table(y_forward),
        "xf": split_table(x_forward),
        "xb": split_table(x_back),
        "yb": split_table(y_back),
        "zb": split_table(z_back),
    }


def halves(value):
    high = value.astype(BF16)
    return high, (value - high.astype(F32)).astype(BF16)


def dot(a, b):
    return jnp.dot(a, b, preferred_element_type=F32)


def dot3(a, b):
    return dot(a[0], b[0]) + dot(a[0], b[1]) + dot(a[1], b[0])


def power_of_two(exponent):
    size = jnp.abs(exponent)
    negative = exponent < 0
    result = jnp.ones(exponent.shape, F32)
    for bit in range(7):
        step = 1 << bit
        factor = jnp.where(negative, F32(2.0**-step), F32(2.0**step))
        result = jnp.where((size & step) != 0, result * factor, result)
    return result


def exponent_of(largest):
    log2 = jnp.log(jnp.maximum(largest, 1e-32)) * F32(1.0 / np.log(2.0))
    return (jnp.floor(log2 + 0.001) - 14.0).astype(jnp.int32)


def coded(block, exp_row, residual_lanes=None):
    exponent = exponent_of(jnp.max(jnp.abs(block), axis=0, keepdims=True))
    scaled = block * power_of_two(-exponent)
    whole = jnp.round(scaled)
    if residual_lanes is not None:
        whole = jnp.where(residual_lanes, jnp.round((scaled - whole) * 32768.0), whole)
        exponent = jnp.where(residual_lanes[:1], exponent - 15, exponent)
    rows = lax.broadcasted_iota(jnp.int32, block.shape, 0)
    return jnp.where(rows >= exp_row, exponent, whole.astype(jnp.int32)).astype(jnp.int16)


def decoded(block, exp_row):
    numbers = block.astype(jnp.int32)
    return numbers.astype(F32) * power_of_two(numbers[exp_row : exp_row + 1])


def compact_kernel(occ_ref, psi_ref, out_ref, scratch):
    for step in range(STEPS):
        scratch[...] = jnp.full((ROWS, LANES), occ_ref[0], jnp.int32).astype(F32)
        for group in range(GROUPS):
            tile = (group * STEPS + step) * LANES
            scratch[pl.ds(group, SLAB, stride=GROUPS), :] = psi_ref[:, tile : tile + LANES].astype(F32)
        out_ref[step] = scratch[...].astype(BF16)


def density_kernel(odd_ref, u_ref, p_ref, q_ref, zf, yf, out_ref, dens, mixed, blocks):
    odd = odd_ref[0] == 1
    for step in range(STEPS):
        lanes = slice(step * LANES, (step + 1) * LANES)
        u, p, q = (ref[step].astype(F32) for ref in (u_ref, p_ref, q_ref))
        for pair, value in enumerate((jnp.where(odd, u, q) * p, u * q)):
            dens[pair, 0, :, lanes], dens[pair, 1, :, lanes] = halves(value)
    for pair in range(2):
        for j, (first, offset, count) in enumerate(WINDOWS):
            lanes = slice(first * LANES, (first + count) * LANES)
            rows = slice(112 - offset, 112 - offset + count * LANES)
            mixed[pair, j, :ROWS] = dot3(
                (dens[pair, 0, :, lanes], dens[pair, 1, :, lanes]), (zf[0, rows], zf[1, rows])
            )
    pad = jnp.zeros((64, 256), BF16)
    low_half = lax.broadcasted_iota(jnp.int32, (ROWS, LANES), 1) < 64
    for x in range(SLAB):
        fields = []
        for pair in range(2):
            plane = jnp.concatenate(
                [mixed[pair, j, GROUPS * x : GROUPS * x + 24] for j in range(8)], axis=0
            )
            plane = [jnp.concatenate([half, pad], axis=0) for half in halves(plane)]
            fields.append(dot3((yf[0], yf[1]), plane))
        rest = jnp.where(low_half, fields[0][:, LANES:], fields[1][:, LANES:])
        for part, field in enumerate((fields[0][:, :LANES], fields[1][:, :LANES], rest)):
            for dest in range(FFT):
                start = part * BLOCK + x * SLAB
                blocks[dest, start : start + 16] = field[16 * dest : 16 * dest + 16]
    lane = lax.broadcasted_iota(jnp.int32, (BLOCK, LANES), 1)
    residual = (lane % 64) >= 48
    for dest in range(FFT):
        for part in range(PARTS):
            rows = slice(part * BLOCK, (part + 1) * BLOCK)
            used = lax.broadcasted_iota(jnp.int32, (BLOCK, LANES), 0) < CELLS
            block = jnp.where(used, blocks[dest, rows], 0.0)
            out_ref[dest, rows] = coded(block, EXP_ROW, residual if part == 2 else None)


def expand(in_ref, cells):
    for source in range(FFT):
        for part in range(PARTS):
            rows = slice(part * BLOCK, (part + 1) * BLOCK)
            cells[source, rows] = decoded(in_ref[source, rows], EXP_ROW)
        cells[source, PARTS * BLOCK :] = jnp.zeros((48, LANES), F32)


def gathered(cells, start):
    parts = []
    for part in range(PARTS):
        parts.append(
            jnp.concatenate(
                [cells[s, pl.ds(part * BLOCK + start, 16, stride=SLAB), :] for s in range(FFT)],
                axis=0,
            )
        )
    return jnp.concatenate(parts, axis=1)


def filter_kernel(in_ref, w_ref, xf, xb, out_ref, cells, blocks):
    expand(in_ref, cells)
    pad = jnp.zeros((ROWS - NG, PARTS * LANES), BF16)
    for ky in range(SLAB):
        spectrum = dot3((xf[0], xf[1]), halves(gathered(cells, ky)))
        weight = w_ref[ky]
        spectrum = spectrum * jnp.concatenate([weight[:, :LANES], weight], axis=1)
        field = dot3(
            (xb[0], xb[1]), [jnp.concatenate([half, pad], axis=0) for half in halves(spectrum)]
        )
        for part in range(PARTS):
            for dest in range(FFT):
                start = part * BLOCK + ky * SLAB
                blocks[dest, start : start + 16] = field[
                    16 * dest : 16 * dest + 16, part * LANES : (part + 1) * LANES
                ]
    used = lax.broadcasted_iota(jnp.int32, (BLOCK, LANES), 0) < CELLS
    for dest in range(FFT):
        for part in range(PARTS):
            rows = slice(part * BLOCK, (part + 1) * BLOCK)
            out_ref[dest, rows] = coded(jnp.where(used, blocks[dest, rows], 0.0), EXP_ROW)


def product_kernel(
    odd_ref, in_ref, u_ref, p_ref, q_ref, yb, zb, own_ref, to_y, to_z, cells, mixed
):
    expand(in_ref, cells)
    for x in range(SLAB):
        plane = dot3((yb[0], yb[1]), halves(gathered(cells, x)))
        for j in range(8):
            mixed[j, GROUPS * x : GROUPS * x + 24] = plane[24 * j : 24 * j + 24]
    odd = odd_ref[0] == 1

    def occupation(ref):
        return -0.5 * ref[0, 240:256].astype(F32)[8:9]

    f_u, f_p, f_q = occupation(u_ref), occupation(p_ref), occupation(q_ref)
    f_r = jnp.where(odd, f_u, f_q)
    f_own, f_send = jnp.where(odd, f_p, 0.0), jnp.where(odd, 0.0, f_p)
    pending = [[], []]

    def finish(step, v1, v2):
        u, p, q = (ref[step].astype(F32) for ref in (u_ref, p_ref, q_ref))
        v1p = v1 * p
        own_ref[step] = f_q * (v2 * q) + f_own * v1p
        to_y[step] = coded(f_r * (v1 * jnp.where(odd, u, q)), 242)
        to_z[step] = coded(f_u * (v2 * u) + f_send * v1p, 242)

    carried = {}
    used = lax.broadcasted_iota(jnp.int32, (ROWS, LANES), 0) < 242
    for j, (first, _, count) in enumerate(WINDOWS):
        rows = jnp.concatenate([mixed[j, :ROWS]], axis=0)
        rows = jnp.where(
            lax.broadcasted_iota(jnp.int32, (ROWS, PARTS * LANES), 0) < 242, rows, 0.0
        )
        high, low = halves(rows)
        width = slice(0, count * LANES)
        fields = []
        for pair in range(2):
            lhs = [
                jnp.concatenate(
                    [half[:, pair * LANES : (pair + 1) * LANES], half[:, 2 * LANES :]], axis=1
                )
                for half in (high, low)
            ]
            if pair == 0:
                rhs = [
                    jnp.concatenate([zb[h, j, 0:128, width], zb[h, j, 192:320, width]], axis=0)
                    for h in range(2)
                ]
            else:
                rhs = [zb[h, j, 0:256, width] for h in range(2)]
            fields.append(dot3(lhs, rhs))
        for k in range(count):
            step = first + k
            pieces = [field[:, k * LANES : (k + 1) * LANES] for field in fields]
            if step in carried:
                pieces = [a + b for a, b in zip(carried[step], pieces)]
            carried[step] = pieces
        limit = WINDOWS[j + 1][0] if j < 7 else STEPS
        for step in sorted(carried):
            if step < limit:
                finish(step, *carried.pop(step))


def sum_kernel(own_ref, y_ref, z_ref, out_ref, scratch):
    for step in range(STEPS):
        scratch[...] = own_ref[step] + decoded(y_ref[step], 242) + decoded(z_ref[step], 242)
        for group in range(GROUPS):
            tile = (group * STEPS + step) * LANES
            out_ref[:, tile : tile + LANES] = scratch[pl.ds(group, SLAB, stride=GROUPS), :]


VMEM = pl.BlockSpec(memory_space=pltpu.VMEM)
SMEM = pl.BlockSpec(memory_space=pltpu.SMEM)


def call(kernel, outs, in_specs, scratch, args, flops):
    shapes = [jax.ShapeDtypeStruct(*o) for o in outs]
    moved = sum(int(np.prod(a.shape)) * a.dtype.itemsize for a in list(args) + shapes)
    single = len(outs) == 1
    return pl.pallas_call(
        kernel,
        out_shape=shapes[0] if single else shapes,
        in_specs=in_specs,
        out_specs=VMEM if single else [VMEM] * len(outs),
        scratch_shapes=scratch,
        compiler_params=pltpu.CompilerParams(vmem_limit_bytes=56 * 1024 * 1024),
        cost_estimate=pl.CostEstimate(flops=flops, bytes_accessed=moved, transcendentals=0),
    )(*args)


def kernel_weights():
    def squares(indices):
        folded = jnp.minimum(indices, NG - indices).astype(F32)
        return folded * folded

    kx = squares(jnp.arange(NG, dtype=jnp.int32))
    ky = squares(lax.axis_index("fft") * SLAB + jnp.arange(SLAB, dtype=jnp.int32))
    kz = squares(jnp.asarray(KZ_FIRST + KZ_REST + KZ_REST, jnp.int32))
    summed = ky[:, None, None] + kx[None, :, None] + kz[None, None, :]
    safe = jnp.maximum(summed, 1.0)
    radius = jnp.sqrt(safe)
    profile = 2.0 * (1.0 - jnp.cos(jnp.pi * radius)) / (jnp.pi * jnp.pi * safe)
    return jnp.where(summed > 0.5, profile, 1.0) * (0.25 / float(NG) ** 1.5)


def shards(wavefunctions, band_occ):
    size = lax.axis_size("band")
    swap = [(g, g ^ 1) for g in range(size)]
    there = [(g, (g - 2 if g % 2 == 0 else g + 2) % size) for g in range(size)]
    back = [(dest, source) for source, dest in there]
    odd = (lax.axis_index("band") % 2).astype(jnp.int32).reshape(1)
    table = {name: jnp.asarray(value) for name, value in tables().items()}
    layout = (STEPS, ROWS, LANES)
    payload = ((FFT, PARTS * BLOCK, LANES), jnp.int16)
    cells = pltpu.VMEM((FFT, PARTS * BLOCK + 48, LANES), F32)
    blocks = pltpu.VMEM((FFT, PARTS * BLOCK, LANES), F32)

    u = call(
        compact_kernel, [(layout, BF16)], [SMEM, VMEM],
        [pltpu.VMEM((ROWS, LANES), F32)], (band_occ, wavefunctions[0]), 0,
    )
    q = lax.ppermute(u, "band", there)
    p = lax.ppermute(u, "band", swap)
    weights = kernel_weights()
    sent = call(
        density_kernel, [payload], [SMEM] + [VMEM] * 5,
        [
            pltpu.VMEM((2, 2, ROWS, STEPS * LANES), BF16),
            pltpu.VMEM((2, 8, ROWS + 8, 256), F32),
            blocks,
        ],
        (odd, u, p, q, table["zf"], table["yf"]), 10**9,
    )
    columns = lax.all_to_all(sent, "fft", split_axis=0, concat_axis=0, tiled=True)
    filtered = call(
        filter_kernel, [payload], [VMEM] * 4, [cells, blocks],
        (columns, weights, table["xf"], table["xb"]), 10**9,
    )
    slabs = lax.all_to_all(filtered, "fft", split_axis=0, concat_axis=0, tiled=True)
    own, to_y, to_z = call(
        product_kernel, [(layout, F32), (layout, jnp.int16), (layout, jnp.int16)],
        [SMEM] + [VMEM] * 6,
        [cells, pltpu.VMEM((8, ROWS + 8, PARTS * LANES), F32)],
        (odd, slabs, u, p, q, table["yb"], table["zb"]), 10**9,
    )
    from_z = lax.ppermute(to_z, "band", back)
    from_y = lax.ppermute(to_y, "band", swap)
    result = call(
        sum_kernel, [((SLAB, NG * NG), F32)], [VMEM] * 3,
        [pltpu.VMEM((ROWS, LANES), F32)], (own, from_y, from_z), 0,
    )
    return result[None]


def solution(mesh):
    in_specs = (P("band", "fft", None), P("band"))
    out_specs = P("band", "fft", None)
    return jax.shard_map(shards, mesh=mesh, in_specs=in_specs, out_specs=out_specs, check_vma=False)
```

profile of v0, /device:TPU:1, one launch (start us, length us, event | category | flops | bytes accessed | tf_op | source)
XLA Modules:
  0.0 142.8 jit_solution(14407125621178762669)
XLA Ops:
  0.7 2.4 %shard_map.91.u_ref = bf16[11,256,128]{2,1,0:T(8,128)(2,1)} custom-call(s32[1]{0:T(128)S(6)} %copy.11.occ_ref, bf16[11,30976]{1,0:T(8,128)(2,1)} %bitcast.4), custom_call_target="tpu_custom_call" | custom-call | bytes 1402372 | tf_op jit(solution)/shard_map/pallas_call | solution.py:291
  3.0 6.4 %collective-permute-start.1 = (bf16[11,256,128]{2,1,0:T(8,128)(2,1)}, bf16[11,256,128]{2,1,0:T(8,128)(2,1)S(1)}, u32[]{:S(2)}, u32[]{:S(2)}) collective-permute-start(bf16[11,256,128]{2,1,0:T(8,128)(2,1)} %shard_map.91.u_ref), channel_id=1, source_target_pairs={{0,224},{16,48},{32,0},{48,80},{64,32},{80,112},{96,64},{112,144},... | collective-permute-start | bytes 2162696 | tf_op jit(solution)/shard_map/ppermute | solution.py:333
  9.4 0.0 collective-permute-start
  9.4 15.1 %collective-permute-done.1.q_ref = bf16[11,256,128]{2,1,0:T(8,128)(2,1)S(1)} collective-permute-done((bf16[11,256,128]{2,1,0:T(8,128)(2,1)}, bf16[11,256,128]{2,1,0:T(8,128)(2,1)S(1)}, u32[]{:S(2)}, u32[]{:S(2)}) %collective-permute-start.1) | collective-permute-done | bytes 720928 | tf_op jit(solution)/shard_map/ppermute | solution.py:333
  24.6 0.0 copy-start.1
  24.6 1.8 %collective-permute-done.p_ref = bf16[11,256,128]{2,1,0:T(8,128)(2,1)S(1)} collective-permute-done((bf16[11,256,128]{2,1,0:T(8,128)(2,1)}, bf16[11,256,128]{2,1,0:T(8,128)(2,1)S(1)}, u32[]{:S(2)}, u32[]{:S(2)}) %collective-permute-start) | collective-permute-done | bytes 720928 | tf_op jit(solution)/shard_map/ppermute | solution.py:334
  26.3 0.0 copy-start.2
  26.3 0.0 copy-done.1
  26.3 0.9 copy-done.2
  27.2 8.4 %shard_map.92 = s16[16,384,128]{2,1,0:T(8,128)(2,1)} custom-call(s32[1]{0:T(128)} %bitcast.odd_ref, bf16[11,256,128]{2,1,0:T(8,128)(2,1)} %shard_map.91.u_ref, bf16[11,256,128]{2,1,0:T(8,128)(2,1)} %copy-done.2, bf16[11,256,128]{2,1,0:T(8,128)(2,1)} %copy-done.1, bf16[2,400,256]{2,1,0:T(8,128)(2,1)} %constant.53.clone.zf, bf16[2,256,256]{2,1,0:T(8,128)(2,1)} %constant.54.clone.yf), custom_call_target="tpu_custom_call" | custom-call | flops 1000000000 | bytes 4407300 | tf_op jit(solution)/shard_map/pallas_call | solution.py:291
  35.7 0.0 copy-start.5
  35.7 8.9 %all-to-all-start = ((s16[16,384,128]{2,1,0:T(8,128)(2,1)}), s16[16,384,128]{2,1,0:T(8,128)(2,1)S(1)}, u32[]{:S(2)}, u32[]{:S(2)}) async-start(s16[16,384,128]{2,1,0:T(8,128)(2,1)} %shard_map.92), calls=%async_computation | async-start | bytes 3145728 | tf_op jit(solution)/shard_map/all_to_all | solution.py:345
  44.6 0.1 broadcast_add_fusion
  44.7 0.0 copy-done.5
  44.7 8.6 %fusion.8.w_ref = f32[11,176,256]{2,1,0:T(8,128)} fusion(f32[256]{0:T(256)S(1)} %copy-done.5, f32[11,176]{1,0:T(8,128)S(1)} %broadcast_add_fusion), kind=kLoop, calls=%fused_computation.10 | loop fusion | flops 4956160 | bytes 1991232 | tf_op jit(solution)/shard_map/mul | solution.py:314
  53.3 14.3 %all-to-all-done.in_ref = s16[16,384,128]{2,1,0:T(8,128)(2,1)S(1)} async-done(((s16[16,384,128]{2,1,0:T(8,128)(2,1)}), s16[16,384,128]{2,1,0:T(8,128)(2,1)S(1)}, u32[]{:S(2)}, u32[]{:S(2)}) %all-to-all-start) | async-done | bytes 1572896 | tf_op jit(solution)/shard_map/all_to_all | solution.py:345
  67.6 0.0 copy-start
  67.6 1.1 copy-done
  68.7 9.9 %shard_map.93 = s16[16,384,128]{2,1,0:T(8,128)(2,1)} custom-call(s16[16,384,128]{2,1,0:T(8,128)(2,1)} %copy-done, f32[11,176,256]{2,1,0:T(8,128)} %fusion.8.w_ref, bf16[2,176,256]{2,1,0:T(8,128)(2,1)} %constant.55.clone.xf, bf16[2,256,256]{2,1,0:T(8,128)(2,1)} %constant.56.clone.xb), custom_call_target="tpu_custom_call" | custom-call | flops 1000000000 | bytes 5570560 | tf_op jit(solution)/shard_map/pallas_call | solution.py:291
  78.6 27.7 %all_to_all.10.in_ref = s16[16,384,128]{2,1,0:T(8,128)(2,1)} all-to-all(s16[16,384,128]{2,1,0:T(8,128)(2,1)} %shard_map.93), channel_id=1, replica_groups=mesh['band'=16,'fft'=16] {'fft'}, dimensions={0} | all-to-all | bytes 3145728 | tf_op jit(solution)/shard_map/all_to_all | solution.py:350
  106.3 9.9 %shard_map.94 = (f32[11,256,128]{2,1,0:T(8,128)}, s16[11,256,128]{2,1,0:T(8,128)(2,1)}, s16[11,256,128]{2,1,0:T(8,128)(2,1)}) custom-call(s32[1]{0:T(128)} %bitcast.odd_ref, s16[16,384,128]{2,1,0:T(8,128)(2,1)} %all_to_all.10.in_ref, bf16[11,256,128]{2,1,0:T(8,128)(2,1)} %shard_map.91.u_ref, bf16[11,256,128]{2,1,0:T(8,128)(2,1)} %copy-done.2, ...), custom_call_target="tpu_custom_call" | custom-call | flops 1000000000 | bytes 10747908 | tf_op jit(solution)/shard_map/pallas_call | solution.py:291
  116.2 0.0 collective-permute-start.2
  116.2 0.0 collective-permute-start.3
  116.2 16.8 %collective-permute-done.2.y_ref = s16[11,256,128]{2,1,0:T(8,128)(2,1)S(1)} collective-permute-done((s16[11,256,128]{2,1,0:T(8,128)(2,1)}, s16[11,256,128]{2,1,0:T(8,128)(2,1)S(1)}, u32[]{:S(2)}, u32[]{:S(2)}) %collective-permute-start.2) | collective-permute-done | bytes 720928 | tf_op jit(solution)/shard_map/ppermute | solution.py:358
  133.0 0.0 copy-start.3
  133.0 1.2 collective-permute-done.3.z_ref
  134.2 0.0 copy-start.4
  134.2 0.0 copy-done.3
  134.2 0.9 copy-done.4
  135.1 3.7 %shard_map.95 = f32[11,30976]{1,0:T(8,128)} custom-call(f32[11,256,128]{2,1,0:T(8,128)} %get-tuple-element.8.own_ref, s16[11,256,128]{2,1,0:T(8,128)(2,1)} %copy-done.3, s16[11,256,128]{2,1,0:T(8,128)(2,1)} %copy-done.4), custom_call_target="tpu_custom_call" | custom-call | bytes 4246528 | tf_op jit(solution)/shard_map/pallas_call | solution.py:291
  138.8 4.0 %copy.10 = f32[1,11,30976]{2,0,1:T(1,128)} copy(f32[1,11,30976]{2,1,0:T(8,128)} %bitcast.3) | data formatting | bytes 2725888 | tf_op jit(solution)/shard_map/broadcast_in_dim | solution.py:363
  (2 shorter events, 0.0 us)
Async XLA Ops:
  3.0 21.5 %collective-permute-start.1 = (bf16[11,256,128]{2,1,0:T(8,128)(2,1)}, bf16[11,256,128]{2,1,0:T(8,128)(2,1)S(1)}, u32[]{:S(2)}, u32[]{:S(2)}) collective-permute-start(bf16[11,256,128]{2,1,0:T(8,128)(2,1)} %shard_map.91.u_ref), channel_id=1, source_target_pairs={{0,224},{16,48},{32,0},{48,80},{64,32},{80,112},{96,64},{112,144},... | collective-permute-start | bytes 2162696 | tf_op jit(solution)/shard_map/ppermute | solution.py:333
  9.4 16.9 %collective-permute-start = (bf16[11,256,128]{2,1,0:T(8,128)(2,1)}, bf16[11,256,128]{2,1,0:T(8,128)(2,1)S(1)}, u32[]{:S(2)}, u32[]{:S(2)}) collective-permute-start(bf16[11,256,128]{2,1,0:T(8,128)(2,1)} %shard_map.91.u_ref), channel_id=1, source_target_pairs={{0,16},{16,0},{32,48},{48,32},{64,80},{80,64},{96,112},{112,96},{1... | collective-permute-start | bytes 2162696 | tf_op jit(solution)/shard_map/ppermute | solution.py:334
  24.6 1.8 %copy-start.1 = (bf16[11,256,128]{2,1,0:T(8,128)(2,1)}, bf16[11,256,128]{2,1,0:T(8,128)(2,1)S(1)}, u32[]{:S(2)}) copy-start(bf16[11,256,128]{2,1,0:T(8,128)(2,1)S(1)} %collective-permute-done.1.q_ref) | copy-start | bytes 2162692
  26.3 0.9 copy-start.2
  35.7 9.0 %copy-start.5 = (f32[256]{0:T(256)S(1)}, f32[256]{0:T(256)}, u32[]{:S(2)}) copy-start(f32[256]{0:T(256)} %constant.66) | copy-start | bytes 3076
  35.7 31.9 %all-to-all-start = ((s16[16,384,128]{2,1,0:T(8,128)(2,1)}), s16[16,384,128]{2,1,0:T(8,128)(2,1)S(1)}, u32[]{:S(2)}, u32[]{:S(2)}) async-start(s16[16,384,128]{2,1,0:T(8,128)(2,1)} %shard_map.92), calls=%async_computation | async-start | bytes 3145728 | tf_op jit(solution)/shard_map/all_to_all | solution.py:345
  67.6 1.1 copy-start
  116.2 16.8 %collective-permute-start.2 = (s16[11,256,128]{2,1,0:T(8,128)(2,1)}, s16[11,256,128]{2,1,0:T(8,128)(2,1)S(1)}, u32[]{:S(2)}, u32[]{:S(2)}) collective-permute-start(s16[11,256,128]{2,1,0:T(8,128)(2,1)} %get-tuple-element.9), channel_id=1, source_target_pairs={{0,16},{16,0},{32,48},{48,32},{64,80},{80,64},{96,112},{112,96},{1... | collective-permute-start | bytes 2162696 | tf_op jit(solution)/shard_map/ppermute | solution.py:358
  116.2 18.0 %collective-permute-start.3 = (s16[11,256,128]{2,1,0:T(8,128)(2,1)}, s16[11,256,128]{2,1,0:T(8,128)(2,1)S(1)}, u32[]{:S(2)}, u32[]{:S(2)}) collective-permute-start(s16[11,256,128]{2,1,0:T(8,128)(2,1)} %get-tuple-element.10), channel_id=1, source_target_pairs={{224,0},{48,16},{0,32},{80,48},{32,64},{112,80},{64,96},{144,112},... | collective-permute-start | bytes 2162696 | tf_op jit(solution)/shard_map/ppermute | solution.py:357
  133.0 1.2 copy-start.3
  134.2 0.9 copy-start.4
where the time goes:
time: 143 us
  waiting for transfers between devices  49.1 us (34%)
  Pallas kernels  34.3 us (24%)
  blocking collectives  27.7 us (19%)
  starting transfers between devices  15.4 us (11%)
  other arithmetic  8.7 us (6%)
  local copies, waits for them, and re-layouts  6.94 us (5%)
    pallas_call x5, Pallas kernels, call(): pl.pallas_call(kernel, out_shape=shapes[0] if single else shapes, in_spec...  34.3 us
    all_to_all x1, blocking collectives, shards(): lax.all_to_all(filtered, 'fft', split_axis=0, concat_axis=0, tiled=True)  27.7 us
    ppermute x1, waiting for transfers between devices, shards(): from_y = lax.ppermute(to_y, 'band', swap)  16.8 us
    ppermute x1, waiting for transfers between devices, shards(): q = lax.ppermute(u, 'band', there)  15.1 us
    all_to_all x1, waiting for transfers between devices, shards(): lax.all_to_all(sent, 'fft', split_axis=0, concat_axis=0, tiled=True)  14.3 us
    all_to_all x1, starting transfers between devices, shards(): lax.all_to_all(sent, 'fft', split_axis=0, concat_axis=0, tiled=True)  8.94 us
    mul x1, other arithmetic, kernel_weights(): return jnp.where(summed > 0.5, profile, 1.0) * (0.25 / float(NG) ** 1.5)  8.61 us
    ppermute x1, starting transfers between devices, shards(): q = lax.ppermute(u, 'band', there)  6.41 us
  transfers between devices with their start and end apart: 5, of which 5 were waited for; matrix products, arithmetic and copies ran while one was open for 6% of the time, Pallas kernels for 0%

commit v1 on v0

--- a/solution.py
+++ b/solution.py
@@ -128,7 +128,11 @@
         out_ref[step] = scratch[...].astype(BF16)
 
 
-def density_kernel(odd_ref, u_ref, p_ref, q_ref, zf, yf, out_ref, dens, mixed, blocks):
+def density_kernel(
+    odd_ref, u_ref, p_ref, q_ref, zf, yf_ref, out_ref, dens, mixed, blocks, yf, sem
+):
+    copy = pltpu.make_async_copy(yf_ref, yf, sem)
+    copy.start()
     odd = odd_ref[0] == 1
     for step in range(STEPS):
         lanes = slice(step * LANES, (step + 1) * LANES)
@@ -142,6 +146,7 @@
             mixed[pair, j, :ROWS] = dot3(
                 (dens[pair, 0, :, lanes], dens[pair, 1, :, lanes]), (zf[0, rows], zf[1, rows])
             )
+    copy.wait()
     pad = jnp.zeros((64, 256), BF16)
     low_half = lax.broadcasted_iota(jnp.int32, (ROWS, LANES), 1) < 64
     for x in range(SLAB):
@@ -187,8 +192,16 @@
     return jnp.concatenate(parts, axis=1)
 
 
-def filter_kernel(in_ref, w_ref, xf, xb, out_ref, cells, blocks):
+def filter_kernel(in_ref, w_ref, xf_ref, xb_ref, out_ref, cells, blocks, xf, xb, sems):
+    copies = [
+        pltpu.make_async_copy(xf_ref, xf, sems.at[0]),
+        pltpu.make_async_copy(xb_ref, xb, sems.at[1]),
+    ]
+    for copy in copies:
+        copy.start()
     expand(in_ref, cells)
+    for copy in copies:
+        copy.wait()
     pad = jnp.zeros((ROWS - NG, PARTS * LANES), BF16)
     for ky in range(SLAB):
         spectrum = dot3((xf[0], xf[1]), halves(gathered(cells, ky)))
@@ -272,19 +285,18 @@
                 finish(step, *carried.pop(step))
 
 
-def sum_kernel(own_ref, y_ref, z_ref, out_ref, scratch):
+def sum_kernel(own_ref, y_ref, z_ref, out_ref):
     for step in range(STEPS):
-        scratch[...] = own_ref[step] + decoded(y_ref[step], 242) + decoded(z_ref[step], 242)
-        for group in range(GROUPS):
-            tile = (group * STEPS + step) * LANES
-            out_ref[:, tile : tile + LANES] = scratch[pl.ds(group, SLAB, stride=GROUPS), :]
+        total = own_ref[step] + decoded(y_ref[step], 242) + decoded(z_ref[step], 242)
+        out_ref[pl.ds(step, 242, stride=STEPS), 0, :] = total[:242]
 
 
 VMEM = pl.BlockSpec(memory_space=pltpu.VMEM)
 SMEM = pl.BlockSpec(memory_space=pltpu.SMEM)
-
-
-def call(kernel, outs, in_specs, scratch, args, flops):
+ANY = pl.BlockSpec(memory_space=pl.ANY)
+
+
+def call(kernel, outs, in_specs, scratch, args, flops, vmem_mib):
     shapes = [jax.ShapeDtypeStruct(*o) for o in outs]
     moved = sum(int(np.prod(a.shape)) * a.dtype.itemsize for a in list(args) + shapes)
     single = len(outs) == 1
@@ -294,7 +306,7 @@
         in_specs=in_specs,
         out_specs=VMEM if single else [VMEM] * len(outs),
         scratch_shapes=scratch,
-        compiler_params=pltpu.CompilerParams(vmem_limit_bytes=56 * 1024 * 1024),
+        compiler_params=pltpu.CompilerParams(vmem_limit_bytes=vmem_mib * 2**20),
         cost_estimate=pl.CostEstimate(flops=flops, bytes_accessed=moved, transcendentals=0),
     )(*args)
 
@@ -328,39 +340,49 @@
 
     u = call(
         compact_kernel, [(layout, BF16)], [SMEM, VMEM],
-        [pltpu.VMEM((ROWS, LANES), F32)], (band_occ, wavefunctions[0]), 0,
+        [pltpu.VMEM((ROWS, LANES), F32)], (band_occ, wavefunctions[0]), 0, 4,
     )
     q = lax.ppermute(u, "band", there)
     p = lax.ppermute(u, "band", swap)
     weights = kernel_weights()
+    p, weights = lax.optimization_barrier((p, weights))
     sent = call(
-        density_kernel, [payload], [SMEM] + [VMEM] * 5,
+        density_kernel, [payload], [SMEM] + [VMEM] * 4 + [ANY],
         [
             pltpu.VMEM((2, 2, ROWS, STEPS * LANES), BF16),
             pltpu.VMEM((2, 8, ROWS + 8, 256), F32),
             blocks,
+            pltpu.VMEM((2, 256, 256), BF16),
+            pltpu.SemaphoreType.DMA,
         ],
-        (odd, u, p, q, table["zf"], table["yf"]), 10**9,
+        (odd, u, p, q, table["zf"], table["yf"]), 10**9, 20,
     )
     columns = lax.all_to_all(sent, "fft", split_axis=0, concat_axis=0, tiled=True)
     filtered = call(
-        filter_kernel, [payload], [VMEM] * 4, [cells, blocks],
-        (columns, weights, table["xf"], table["xb"]), 10**9,
+        filter_kernel, [payload], [VMEM] * 2 + [ANY] * 2,
+        [
+            cells,
+            blocks,
+            pltpu.VMEM((2, NG, 256), BF16),
+            pltpu.VMEM((2, 256, 256), BF16),
+            pltpu.SemaphoreType.DMA((2,)),
+        ],
+        (columns, weights, table["xf"], table["xb"]), 10**9, 18,
     )
     slabs = lax.all_to_all(filtered, "fft", split_axis=0, concat_axis=0, tiled=True)
     own, to_y, to_z = call(
         product_kernel, [(layout, F32), (layout, jnp.int16), (layout, jnp.int16)],
         [SMEM] + [VMEM] * 6,
         [cells, pltpu.VMEM((8, ROWS + 8, PARTS * LANES), F32)],
-        (odd, slabs, u, p, q, table["yb"], table["zb"]), 10**9,
+        (odd, slabs, u, p, q, table["yb"], table["zb"]), 10**9, 24,
     )
     from_z = lax.ppermute(to_z, "band", back)
     from_y = lax.ppermute(to_y, "band", swap)
     result = call(
-        sum_kernel, [((SLAB, NG * NG), F32)], [VMEM] * 3,
-        [pltpu.VMEM((ROWS, LANES), F32)], (own, from_y, from_z), 0,
-    )
-    return result[None]
+        sum_kernel, [((SLAB * NG * NG // LANES, 1, LANES), F32)], [VMEM] * 3, [],
+        (own, from_y, from_z), 0, 8,
+    )
+    return result.reshape(1, SLAB, NG * NG)
 
 
 def solution(mesh):

time: 143 us -> 122 us (0.85)
  blocking collectives: 27.7 us -> 57.7 us
  waiting for transfers between devices: 49.1 us -> 26.2 us
  Pallas kernels: 34.3 us -> 20.7 us
  starting transfers between devices: 15.4 us -> 6.66 us
  local copies, waits for them, and re-layouts: 6.94 us -> 1.23 us
    all_to_all x0 -> x1, blocking collectives: none -> 31.4 us  [shards(): lax.all_to_all(sent, 'fft', split_axis=0, concat_axis=0, tiled=True)]
    ppermute x1, waiting for transfers between devices: 15.1 us -> 0.01 us  [shards(): q = lax.ppermute(u, 'band', there)]
    all_to_all x1 -> x0, waiting for transfers between devices: 14.3 us -> none  [shards(): lax.all_to_all(sent, 'fft', split_axis=0, concat_axis=0, tiled=True)]
    pallas_call x5, Pallas kernels: 34.3 us -> 20.7 us  [call(): pl.pallas_call(kernel, out_shape=shapes[0] if single else shapes, in_spec...]
    all_to_all x1 -> x0, starting transfers between devices: 8.94 us -> none  [shards(): lax.all_to_all(sent, 'fft', split_axis=0, concat_axis=0, tiled=True)]
    ppermute x1, waiting for transfers between devices: 1.77 us -> 8.39 us  [shards(): p = lax.ppermute(u, 'band', swap)]
    broadcast_in_dim x1 -> x0, local copies, waits for them, and re-layouts: 4.02 us -> none  [shards(): return result[None]]
    unnamed x12 -> x14, local copies, waits for them, and re-layouts: 2.92 us -> 1.23 us
  transfers between devices with their start and end apart: 5 -> 4, of which waited for: 5 -> 3; matrix products, arithmetic and copies ran while one was open for 6% -> 7% of each run, Pallas kernels for 0% -> 0%
where the time goes in v1:
time: 122 us
  blocking collectives  57.7 us (47%)
  waiting for transfers between devices  26.2 us (21%)
  Pallas kernels  20.7 us (17%)
  other arithmetic  8.29 us (7%)
  starting transfers between devices  6.66 us (5%)
  local copies, waits for them, and re-layouts  1.23 us (1%)
    all_to_all x1, blocking collectives, shards(): lax.all_to_all(sent, 'fft', split_axis=0, concat_axis=0, tiled=True)  31.4 us
    all_to_all x1, blocking collectives, shards(): lax.all_to_all(filtered, 'fft', split_axis=0, concat_axis=0, tiled=True)  26.4 us
    pallas_call x5, Pallas kernels, call(): pl.pallas_call(kernel, out_shape=shapes[0] if single else shapes, in_spec...  20.7 us
    ppermute x1, waiting for transfers between devices, shards(): from_y = lax.ppermute(to_y, 'band', swap)  16.5 us
    ppermute x1, waiting for transfers between devices, shards(): p = lax.ppermute(u, 'band', swap)  8.39 us
    mul x1, other arithmetic, kernel_weights(): return jnp.where(summed > 0.5, profile, 1.0) * (0.25 / float(NG) ** 1.5)  8.2 us
    ppermute x1, starting transfers between devices, shards(): q = lax.ppermute(u, 'band', there)  6.48 us
  transfers between devices with their start and end apart: 4, of which 3 were waited for; matrix products, arithmetic and copies ran while one was open for 7% of the time, Pallas kernels for 0%

profile of v1, /device:TPU:1, one launch (start us, length us, event | category | flops | bytes accessed | tf_op | source)
XLA Modules:
  0.0 121.5 jit_solution(3383802331406078349)
XLA Ops:
  0.7 0.0 copy-start.1
  0.7 1.2 copy-done.1
  1.9 0.0 copy-start.2
  1.9 0.0 copy-start.4
  1.9 0.3 shard_map.91.u_ref
  2.2 6.5 %collective-permute-start.1 = (bf16[11,256,128]{2,1,0:T(8,128)(2,1)S(1)}, bf16[11,256,128]{2,1,0:T(8,128)(2,1)S(1)}, u32[]{:S(2)}, u32[]{:S(2)}) collective-permute-start(bf16[11,256,128]{2,1,0:T(8,128)(2,1)S(1)} %shard_map.91.u_ref), channel_id=1, source_target_pairs={{0,224},{16,48},{32,0},{48,80},{64,32},{80,112},{96,64},{112,144},... | collective-permute-start | bytes 2162696 | tf_op jit(solution)/shard_map/ppermute | solution.py:345
  8.7 0.0 collective-permute-start
  8.7 0.1 broadcast_add_fusion
  8.7 8.2 %fusion.8.w_ref = f32[11,176,256]{2,1,0:T(8,128)S(1)} fusion(f32[256]{0:T(256)} %constant.66, f32[11,176]{1,0:T(8,128)S(1)} %broadcast_add_fusion), kind=kLoop, calls=%fused_computation.10 | loop fusion | flops 4956160 | bytes 1991232 | tf_op jit(solution)/shard_map/mul | solution.py:326
  17.0 8.4 %collective-permute-done.p_ref = bf16[11,256,128]{2,1,0:T(8,128)(2,1)S(1)} collective-permute-done((bf16[11,256,128]{2,1,0:T(8,128)(2,1)S(1)}, bf16[11,256,128]{2,1,0:T(8,128)(2,1)S(1)}, u32[]{:S(2)}, u32[]{:S(2)}) %collective-permute-start) | collective-permute-done | bytes 720928 | tf_op jit(solution)/shard_map/ppermute | solution.py:346
  25.3 0.0 collective-permute-done.1.q_ref
  25.3 0.0 copy-done.2
  25.3 0.0 copy-done.4
  25.4 5.9 %shard_map.92 = s16[16,384,128]{2,1,0:T(8,128)(2,1)S(1)} custom-call(s32[1]{0:T(128)} %bitcast.odd_ref, bf16[11,256,128]{2,1,0:T(8,128)(2,1)S(1)} %shard_map.91.u_ref, bf16[11,256,128]{2,1,0:T(8,128)(2,1)S(1)} %collective-permute-done.p_ref, bf16[11,256,128]{2,1,0:T(8,128)(2,1)S(1)} %collective-permute-done.1.q_ref, bf16[2,400,256]{2,1,0:T(8,128)(2,1)S(1)} %copy-done.2, ...), custom_call_target="tpu_custom_call" | custom-call | flops 1000000000 | bytes 4407300 | tf_op jit(solution)/shard_map/pallas_call | solution.py:303
  31.3 0.0 copy-start.3
  31.3 0.0 copy-start.6
  31.3 31.4 %all_to_all.10.in_ref = s16[16,384,128]{2,1,0:T(8,128)(2,1)S(1)} all-to-all(s16[16,384,128]{2,1,0:T(8,128)(2,1)S(1)} %shard_map.92), channel_id=1, replica_groups=mesh['band'=16,'fft'=16] {'fft'}, dimensions={0} | all-to-all | bytes 3145728 | tf_op jit(solution)/shard_map/all_to_all | solution.py:360
  62.6 0.0 copy-done.3
  62.6 0.0 copy-done.6
  62.6 0.0 copy-start
  62.6 7.0 %shard_map.93 = s16[16,384,128]{2,1,0:T(8,128)(2,1)S(1)} custom-call(s16[16,384,128]{2,1,0:T(8,128)(2,1)S(1)} %all_to_all.10.in_ref, f32[11,176,256]{2,1,0:T(8,128)S(1)} %fusion.8.w_ref, bf16[2,176,256]{2,1,0:T(8,128)(2,1)S(1)} %copy-done.6, bf16[2,256,256]{2,1,0:T(8,128)(2,1)S(1)} %copy-done.3), custom_call_target="tpu_custom_call" | custom-call | flops 1000000000 | bytes 5570560 | tf_op jit(solution)/shard_map/pallas_call | solution.py:303
  69.6 0.0 copy-start.5
  69.6 26.4 %all_to_all.11.in_ref = s16[16,384,128]{2,1,0:T(8,128)(2,1)S(1)} all-to-all(s16[16,384,128]{2,1,0:T(8,128)(2,1)S(1)} %shard_map.93), channel_id=1, replica_groups=mesh['band'=16,'fft'=16] {'fft'}, dimensions={0} | all-to-all | bytes 3145728 | tf_op jit(solution)/shard_map/all_to_all | solution.py:372
  96.0 0.0 copy-done
  96.0 0.0 copy-done.5
  96.0 5.3 %shard_map.94 = (f32[11,256,128]{2,1,0:T(8,128)S(1)}, s16[11,256,128]{2,1,0:T(8,128)(2,1)S(1)}, s16[11,256,128]{2,1,0:T(8,128)(2,1)S(1)}) custom-call(s32[1]{0:T(128)} %bitcast.odd_ref, s16[16,384,128]{2,1,0:T(8,128)(2,1)S(1)} %all_to_all.11.in_ref, bf16[11,256,128]{2,1,0:T(8,128)(2,1)S(1)} %shard_map.91.u_ref, ...), custom_call_target="tpu_custom_call" | custom-call | flops 1000000000 | bytes 10747908 | tf_op jit(solution)/shard_map/pallas_call | solution.py:303
  101.4 0.1 collective-permute-start.2
  101.5 0.1 collective-permute-start.3
  101.6 16.5 %collective-permute-done.2.y_ref = s16[11,256,128]{2,1,0:T(8,128)(2,1)S(1)} collective-permute-done((s16[11,256,128]{2,1,0:T(8,128)(2,1)S(1)}, s16[11,256,128]{2,1,0:T(8,128)(2,1)S(1)}, u32[]{:S(2)}, u32[]{:S(2)}) %collective-permute-start.2) | collective-permute-done | bytes 720928 | tf_op jit(solution)/shard_map/ppermute | solution.py:380
  118.0 1.3 %collective-permute-done.3.z_ref = s16[11,256,128]{2,1,0:T(8,128)(2,1)S(1)} collective-permute-done((s16[11,256,128]{2,1,0:T(8,128)(2,1)S(1)}, s16[11,256,128]{2,1,0:T(8,128)(2,1)S(1)}, u32[]{:S(2)}, u32[]{:S(2)}) %collective-permute-start.3) | collective-permute-done | bytes 720928 | tf_op jit(solution)/shard_map/ppermute | solution.py:379
  119.3 2.2 %shard_map.95 = f32[2662,1,128]{2,1,0:T(1,128)} custom-call(f32[11,256,128]{2,1,0:T(8,128)S(1)} %get-tuple-element.12.own_ref, s16[11,256,128]{2,1,0:T(8,128)(2,1)S(1)} %collective-permute-done.2.y_ref, s16[11,256,128]{2,1,0:T(8,128)(2,1)S(1)} %collective-permute-done.3.z_ref), custom_call_target="tpu_custom_call" | custom-call | bytes 4246528 | tf_op jit(solution)/shard_map/pallas_call | solution.py:303
  (2 shorter events, 0.0 us)
Async XLA Ops:
  0.7 1.2 copy-start.1
  1.9 23.5 %copy-start.2 = (bf16[2,400,256]{2,1,0:T(8,128)(2,1)S(1)}, bf16[2,400,256]{2,1,0:T(8,128)(2,1)}, u32[]{:S(2)}) copy-start(bf16[2,400,256]{2,1,0:T(8,128)(2,1)} %constant.53.clone.zf) | copy-start | bytes 1228804
  1.9 23.5 %copy-start.4 = (bf16[2,256,256]{2,1,0:T(8,128)(2,1)S(1)}, bf16[2,256,256]{2,1,0:T(8,128)(2,1)}, u32[]{:S(2)}) copy-start(bf16[2,256,256]{2,1,0:T(8,128)(2,1)} %constant.54.clone.yf_ref) | copy-start | bytes 786436
  2.2 23.2 %collective-permute-start.1 = (bf16[11,256,128]{2,1,0:T(8,128)(2,1)S(1)}, bf16[11,256,128]{2,1,0:T(8,128)(2,1)S(1)}, u32[]{:S(2)}, u32[]{:S(2)}) collective-permute-start(bf16[11,256,128]{2,1,0:T(8,128)(2,1)S(1)} %shard_map.91.u_ref), channel_id=1, source_target_pairs={{0,224},{16,48},{32,0},{48,80},{64,32},{80,112},{96,64},{112,144},... | collective-permute-start | bytes 2162696 | tf_op jit(solution)/shard_map/ppermute | solution.py:345
  8.7 16.7 %collective-permute-start = (bf16[11,256,128]{2,1,0:T(8,128)(2,1)S(1)}, bf16[11,256,128]{2,1,0:T(8,128)(2,1)S(1)}, u32[]{:S(2)}, u32[]{:S(2)}) collective-permute-start(bf16[11,256,128]{2,1,0:T(8,128)(2,1)S(1)} %shard_map.91.u_ref), channel_id=1, source_target_pairs={{0,16},{16,0},{32,48},{48,32},{64,80},{80,64},{96,112},{112,96},{1... | collective-permute-start | bytes 2162696 | tf_op jit(solution)/shard_map/ppermute | solution.py:346
  31.3 31.4 %copy-start.3 = (bf16[2,256,256]{2,1,0:T(8,128)(2,1)S(1)}, bf16[2,256,256]{2,1,0:T(8,128)(2,1)}, u32[]{:S(2)}) copy-start(bf16[2,256,256]{2,1,0:T(8,128)(2,1)} %constant.56.clone.xb_ref) | copy-start | bytes 786436
  31.3 31.4 %copy-start.6 = (bf16[2,176,256]{2,1,0:T(8,128)(2,1)S(1)}, bf16[2,176,256]{2,1,0:T(8,128)(2,1)}, u32[]{:S(2)}) copy-start(bf16[2,176,256]{2,1,0:T(8,128)(2,1)} %constant.55.clone.xf_ref) | copy-start | bytes 540676
  62.6 33.4 %copy-start = (bf16[2,8,320,384]{3,2,1,0:T(8,128)(2,1)S(1)}, bf16[2,8,320,384]{3,2,1,0:T(8,128)(2,1)}, u32[]{:S(2)}) copy-start(bf16[2,8,320,384]{3,2,1,0:T(8,128)(2,1)} %constant.58.clone.zb) | copy-start | bytes 11796484
  69.6 26.4 %copy-start.5 = (bf16[2,192,256]{2,1,0:T(8,128)(2,1)S(1)}, bf16[2,192,256]{2,1,0:T(8,128)(2,1)}, u32[]{:S(2)}) copy-start(bf16[2,192,256]{2,1,0:T(8,128)(2,1)} %constant.57.clone.yb) | copy-start | bytes 589828
  101.4 16.7 %collective-permute-start.2 = (s16[11,256,128]{2,1,0:T(8,128)(2,1)S(1)}, s16[11,256,128]{2,1,0:T(8,128)(2,1)S(1)}, u32[]{:S(2)}, u32[]{:S(2)}) collective-permute-start(s16[11,256,128]{2,1,0:T(8,128)(2,1)S(1)} %get-tuple-element.13), channel_id=1, source_target_pairs={{0,16},{16,0},{32,48},{48,32},{64,80},{80,64},{96,112},{112,96},{1... | collective-permute-start | bytes 2162696 | tf_op jit(solution)/shard_map/ppermute | solution.py:380
  101.5 17.9 %collective-permute-start.3 = (s16[11,256,128]{2,1,0:T(8,128)(2,1)S(1)}, s16[11,256,128]{2,1,0:T(8,128)(2,1)S(1)}, u32[]{:S(2)}, u32[]{:S(2)}) collective-permute-start(s16[11,256,128]{2,1,0:T(8,128)(2,1)S(1)} %get-tuple-element.14), channel_id=1, source_target_pairs={{224,0},{48,16},{0,32},{80,48},{32,64},{112,80},{64,96},{144,112},... | collective-permute-start | bytes 2162696 | tf_op jit(solution)/shard_map/ppermute | solution.py:379

commit v2 on v1

--- a/solution.py
+++ b/solution.py
@@ -16,11 +16,13 @@
 STEPS = 11
 GROUPS = 22
 ROWS = 256
-OCC_ROW = 248
+USED = 242
+SENT = 248
 CELLS = 121
-BLOCK = 128
-EXP_ROW = 121
 PARTS = 3
+BLOCK = 368
+WINDOW = 128
+PLACES = tuple((part * 120, part * 2) for part in range(PARTS))
 F32 = jnp.float32
 BF16 = jnp.bfloat16
 
@@ -103,20 +105,55 @@
     return (jnp.floor(log2 + 0.001) - 14.0).astype(jnp.int32)
 
 
-def coded(block, exp_row, residual_lanes=None):
+def numbers(block, first, count, residual_lanes=None):
+    rows = lax.broadcasted_iota(jnp.int32, block.shape, 0)
+    block = jnp.where((rows >= first) & (rows < first + count), block, 0.0)
     exponent = exponent_of(jnp.max(jnp.abs(block), axis=0, keepdims=True))
     scaled = block * power_of_two(-exponent)
     whole = jnp.round(scaled)
     if residual_lanes is not None:
         whole = jnp.where(residual_lanes, jnp.round((scaled - whole) * 32768.0), whole)
         exponent = jnp.where(residual_lanes[:1], exponent - 15, exponent)
-    rows = lax.broadcasted_iota(jnp.int32, block.shape, 0)
-    return jnp.where(rows >= exp_row, exponent, whole.astype(jnp.int32)).astype(jnp.int16)
-
-
-def decoded(block, exp_row):
-    numbers = block.astype(jnp.int32)
-    return numbers.astype(F32) * power_of_two(numbers[exp_row : exp_row + 1])
+    return jnp.where(rows == first + count, exponent, whole.astype(jnp.int32))
+
+
+def write_block(blocks, dest, out_ref, residual_lanes=None):
+    codes = []
+    for part, (window, first) in enumerate(PLACES):
+        lanes = residual_lanes if part == 2 else None
+        codes.append(numbers(blocks[dest, window : window + WINDOW], first, CELLS, lanes))
+    rows = lax.broadcasted_iota(jnp.int32, (8, LANES), 0)
+    pieces = [codes[0][:120]]
+    for part in (1, 2):
+        earlier = codes[part - 1][120:]
+        pieces.append(jnp.where(rows < 2 * part, earlier, codes[part][:8]))
+        pieces.append(codes[part][8:120] if part == 1 else codes[part][8:])
+    out_ref[dest] = jnp.concatenate(pieces, axis=0).astype(jnp.int16)
+
+
+def read_blocks(in_ref, cells):
+    for source in range(FFT):
+        block = in_ref[source].astype(jnp.int32)
+        for part, (window, first) in enumerate(PLACES):
+            code = block[window : window + WINDOW]
+            scale = power_of_two(code[first + CELLS : first + CELLS + 1])
+            cells[source, part * WINDOW : (part + 1) * WINDOW] = code.astype(F32) * scale
+        cells[source, PARTS * WINDOW :] = jnp.zeros((56, LANES), F32)
+
+
+def store_cells(blocks, dest, part, line, value):
+    start = part * (CELLS + 1) + line * SLAB
+    size = 16 if line < SLAB - 1 else SLAB
+    blocks[dest, start : start + size] = value[:size]
+
+
+def coded(block):
+    return numbers(block, 0, USED)[:SENT].astype(jnp.int16)
+
+
+def decoded(block):
+    code = block.astype(jnp.int32)
+    return code.astype(F32) * power_of_two(code[USED : USED + 1])
 
 
 def compact_kernel(occ_ref, psi_ref, out_ref, scratch):
@@ -125,7 +162,7 @@
         for group in range(GROUPS):
             tile = (group * STEPS + step) * LANES
             scratch[pl.ds(group, SLAB, stride=GROUPS), :] = psi_ref[:, tile : tile + LANES].astype(F32)
-        out_ref[step] = scratch[...].astype(BF16)
+        out_ref[step] = scratch[:SENT].astype(BF16)
 
 
 def density_kernel(
@@ -138,6 +175,7 @@
         lanes = slice(step * LANES, (step + 1) * LANES)
         u, p, q = (ref[step].astype(F32) for ref in (u_ref, p_ref, q_ref))
         for pair, value in enumerate((jnp.where(odd, u, q) * p, u * q)):
+            value = jnp.concatenate([value, jnp.zeros((ROWS - SENT, LANES), F32)], axis=0)
             dens[pair, 0, :, lanes], dens[pair, 1, :, lanes] = halves(value)
     for pair in range(2):
         for j, (first, offset, count) in enumerate(WINDOWS):
@@ -160,32 +198,19 @@
         rest = jnp.where(low_half, fields[0][:, LANES:], fields[1][:, LANES:])
         for part, field in enumerate((fields[0][:, :LANES], fields[1][:, :LANES], rest)):
             for dest in range(FFT):
-                start = part * BLOCK + x * SLAB
-                blocks[dest, start : start + 16] = field[16 * dest : 16 * dest + 16]
-    lane = lax.broadcasted_iota(jnp.int32, (BLOCK, LANES), 1)
-    residual = (lane % 64) >= 48
+                store_cells(blocks, dest, part, x, field[16 * dest : 16 * dest + 16])
+    residual = (lax.broadcasted_iota(jnp.int32, (WINDOW, LANES), 1) % 64) >= 48
     for dest in range(FFT):
-        for part in range(PARTS):
-            rows = slice(part * BLOCK, (part + 1) * BLOCK)
-            used = lax.broadcasted_iota(jnp.int32, (BLOCK, LANES), 0) < CELLS
-            block = jnp.where(used, blocks[dest, rows], 0.0)
-            out_ref[dest, rows] = coded(block, EXP_ROW, residual if part == 2 else None)
-
-
-def expand(in_ref, cells):
-    for source in range(FFT):
-        for part in range(PARTS):
-            rows = slice(part * BLOCK, (part + 1) * BLOCK)
-            cells[source, rows] = decoded(in_ref[source, rows], EXP_ROW)
-        cells[source, PARTS * BLOCK :] = jnp.zeros((48, LANES), F32)
+        write_block(blocks, dest, out_ref, residual)
 
 
 def gathered(cells, start):
     parts = []
-    for part in range(PARTS):
+    for part, (_, first) in enumerate(PLACES):
+        begin = part * WINDOW + first + start
         parts.append(
             jnp.concatenate(
-                [cells[s, pl.ds(part * BLOCK + start, 16, stride=SLAB), :] for s in range(FFT)],
+                [cells[s, pl.ds(begin, 16, stride=SLAB), :] for s in range(FFT)],
                 axis=0,
             )
         )
@@ -199,34 +224,33 @@
     ]
     for copy in copies:
         copy.start()
-    expand(in_ref, cells)
+    read_blocks(in_ref, cells)
     for copy in copies:
         copy.wait()
-    pad = jnp.zeros((ROWS - NG, PARTS * LANES), BF16)
-    for ky in range(SLAB):
-        spectrum = dot3((xf[0], xf[1]), halves(gathered(cells, ky)))
-        weight = w_ref[ky]
-        spectrum = spectrum * jnp.concatenate([weight[:, :LANES], weight], axis=1)
+    for line in range(0, SLAB, 2):
+        lines = range(line, min(line + 2, SLAB))
+        columns = jnp.concatenate([gathered(cells, ky) for ky in lines], axis=1)
+        spectrum = dot3((xf[0], xf[1]), halves(columns))
+        weight = [w_ref[ky] for ky in lines]
+        weight = [tile for w in weight for tile in (w[:, :LANES], w)]
+        spectrum = spectrum * jnp.concatenate(weight, axis=1)
+        pad = jnp.zeros((ROWS - NG, spectrum.shape[1]), BF16)
         field = dot3(
             (xb[0], xb[1]), [jnp.concatenate([half, pad], axis=0) for half in halves(spectrum)]
         )
-        for part in range(PARTS):
-            for dest in range(FFT):
-                start = part * BLOCK + ky * SLAB
-                blocks[dest, start : start + 16] = field[
-                    16 * dest : 16 * dest + 16, part * LANES : (part + 1) * LANES
-                ]
-    used = lax.broadcasted_iota(jnp.int32, (BLOCK, LANES), 0) < CELLS
+        for place, ky in enumerate(lines):
+            for part in range(PARTS):
+                lanes = slice((place * PARTS + part) * LANES, (place * PARTS + part + 1) * LANES)
+                for dest in range(FFT):
+                    store_cells(blocks, dest, part, ky, field[16 * dest : 16 * dest + 16, lanes])
     for dest in range(FFT):
-        for part in range(PARTS):
-            rows = slice(part * BLOCK, (part + 1) * BLOCK)
-            out_ref[dest, rows] = coded(jnp.where(used, blocks[dest, rows], 0.0), EXP_ROW)
+        write_block(blocks, dest, out_ref)
 
 
 def product_kernel(
     odd_ref, in_ref, u_ref, p_ref, q_ref, yb, zb, own_ref, to_y, to_z, cells, mixed
 ):
-    expand(in_ref, cells)
+    read_blocks(in_ref, cells)
     for x in range(SLAB):
         plane = dot3((yb[0], yb[1]), halves(gathered(cells, x)))
         for j in range(8):
@@ -234,28 +258,23 @@
     odd = odd_ref[0] == 1
 
     def occupation(ref):
-        return -0.5 * ref[0, 240:256].astype(F32)[8:9]
+        return -0.5 * ref[0].astype(F32)[SENT - 1 : SENT]
 
     f_u, f_p, f_q = occupation(u_ref), occupation(p_ref), occupation(q_ref)
     f_r = jnp.where(odd, f_u, f_q)
     f_own, f_send = jnp.where(odd, f_p, 0.0), jnp.where(odd, 0.0, f_p)
-    pending = [[], []]
 
     def finish(step, v1, v2):
         u, p, q = (ref[step].astype(F32) for ref in (u_ref, p_ref, q_ref))
         v1p = v1 * p
         own_ref[step] = f_q * (v2 * q) + f_own * v1p
-        to_y[step] = coded(f_r * (v1 * jnp.where(odd, u, q)), 242)
-        to_z[step] = coded(f_u * (v2 * u) + f_send * v1p, 242)
+        to_y[step] = coded(f_r * (v1 * jnp.where(odd, u, q)))
+        to_z[step] = coded(f_u * (v2 * u) + f_send * v1p)
 
     carried = {}
-    used = lax.broadcasted_iota(jnp.int32, (ROWS, LANES), 0) < 242
+    used = lax.broadcasted_iota(jnp.int32, (ROWS, PARTS * LANES), 0) < USED
     for j, (first, _, count) in enumerate(WINDOWS):
-        rows = jnp.concatenate([mixed[j, :ROWS]], axis=0)
-        rows = jnp.where(
-            lax.broadcasted_iota(jnp.int32, (ROWS, PARTS * LANES), 0) < 242, rows, 0.0
-        )
-        high, low = halves(rows)
+        high, low = halves(jnp.where(used, mixed[j, :ROWS], 0.0))
         width = slice(0, count * LANES)
         fields = []
         for pair in range(2):
@@ -275,7 +294,7 @@
             fields.append(dot3(lhs, rhs))
         for k in range(count):
             step = first + k
-            pieces = [field[:, k * LANES : (k + 1) * LANES] for field in fields]
+            pieces = [field[:SENT, k * LANES : (k + 1) * LANES] for field in fields]
             if step in carried:
                 pieces = [a + b for a, b in zip(carried[step], pieces)]
             carried[step] = pieces
@@ -285,10 +304,24 @@
                 finish(step, *carried.pop(step))
 
 
-def sum_kernel(own_ref, y_ref, z_ref, out_ref):
-    for step in range(STEPS):
-        total = own_ref[step] + decoded(y_ref[step], 242) + decoded(z_ref[step], 242)
-        out_ref[pl.ds(step, 242, stride=STEPS), 0, :] = total[:242]
+def sum_kernel(own_ref, y_ref, z_ref, out_ref, total, sems):
+    scales = [
+        [power_of_two(ref[step].astype(jnp.int32)[USED : USED + 1]) for ref in (y_ref, z_ref)]
+        for step in range(STEPS)
+    ]
+    copies = []
+    for chunk, start in enumerate(range(0, USED, 64)):
+        size = min(64, USED - start)
+        for step in range(STEPS):
+            value = own_ref[step, start : start + size]
+            for ref, scale in zip((y_ref, z_ref), scales[step]):
+                value += ref[step, start : start + 64].astype(jnp.int32).astype(F32)[:size] * scale
+            total[pl.ds(start * STEPS + step, size, stride=STEPS), 0, :] = value
+        rows = pl.ds(start * STEPS, size * STEPS)
+        copies.append(pltpu.make_async_copy(total.at[rows], out_ref.at[rows], sems.at[chunk]))
+        copies[-1].start()
+    for copy in copies:
+        copy.wait()
 
 
 VMEM = pl.BlockSpec(memory_space=pltpu.VMEM)
@@ -296,7 +329,7 @@
 ANY = pl.BlockSpec(memory_space=pl.ANY)
 
 
-def call(kernel, outs, in_specs, scratch, args, flops, vmem_mib):
+def call(kernel, outs, in_specs, scratch, args, flops, vmem_mib, out_spec=VMEM):
     shapes = [jax.ShapeDtypeStruct(*o) for o in outs]
     moved = sum(int(np.prod(a.shape)) * a.dtype.itemsize for a in list(args) + shapes)
     single = len(outs) == 1
@@ -304,7 +337,7 @@
         kernel,
         out_shape=shapes[0] if single else shapes,
         in_specs=in_specs,
-        out_specs=VMEM if single else [VMEM] * len(outs),
+        out_specs=out_spec if single else [out_spec] * len(outs),
         scratch_shapes=scratch,
         compiler_params=pltpu.CompilerParams(vmem_limit_bytes=vmem_mib * 2**20),
         cost_estimate=pl.CostEstimate(flops=flops, bytes_accessed=moved, transcendentals=0),
@@ -333,10 +366,10 @@
     back = [(dest, source) for source, dest in there]
     odd = (lax.axis_index("band") % 2).astype(jnp.int32).reshape(1)
     table = {name: jnp.asarray(value) for name, value in tables().items()}
-    layout = (STEPS, ROWS, LANES)
-    payload = ((FFT, PARTS * BLOCK, LANES), jnp.int16)
-    cells = pltpu.VMEM((FFT, PARTS * BLOCK + 48, LANES), F32)
-    blocks = pltpu.VMEM((FFT, PARTS * BLOCK, LANES), F32)
+    layout = (STEPS, SENT, LANES)
+    payload = ((FFT, BLOCK, LANES), jnp.int16)
+    cells = pltpu.VMEM((FFT, PARTS * WINDOW + 56, LANES), F32)
+    blocks = pltpu.VMEM((FFT, BLOCK, LANES), F32)
 
     u = call(
         compact_kernel, [(layout, BF16)], [SMEM, VMEM],
@@ -379,8 +412,9 @@
     from_z = lax.ppermute(to_z, "band", back)
     from_y = lax.ppermute(to_y, "band", swap)
     result = call(
-        sum_kernel, [((SLAB * NG * NG // LANES, 1, LANES), F32)], [VMEM] * 3, [],
-        (own, from_y, from_z), 0, 8,
+        sum_kernel, [((SLAB * NG * NG // LANES, 1, LANES), F32)], [VMEM] * 3,
+        [pltpu.VMEM((SLAB * NG * NG // LANES, 1, LANES), F32), pltpu.SemaphoreType.DMA((4,))],
+        (own, from_y, from_z), 0, 8, ANY,
     )
     return result.reshape(1, SLAB, NG * NG)
 

time: 122 us -> 117 us (0.959)
  Pallas kernels: 20.7 us -> 18.8 us
  blocking collectives: 57.7 us -> 56.1 us
  waiting for transfers between devices: 26.2 us -> 24.9 us
    pallas_call x5, Pallas kernels: 20.7 us -> 18.8 us  [call(): pl.pallas_call(kernel, out_shape=shapes[0] if single else shapes, in_spec...]
where the time goes in v2:
time: 117 us
  blocking collectives  56.1 us (48%)
  waiting for transfers between devices  24.9 us (21%)
  Pallas kernels  18.8 us (16%)
  other arithmetic  8.28 us (7%)
  starting transfers between devices  6.66 us (6%)
  local copies, waits for them, and re-layouts  1.23 us (1%)
    all_to_all x1, blocking collectives, shards(): lax.all_to_all(sent, 'fft', split_axis=0, concat_axis=0, tiled=True)  30.4 us
    all_to_all x1, blocking collectives, shards(): lax.all_to_all(filtered, 'fft', split_axis=0, concat_axis=0, tiled=True)  25.7 us
    pallas_call x5, Pallas kernels, call(): pl.pallas_call(kernel, out_shape=shapes[0] if single else shapes, in_spec...  18.8 us
    ppermute x1, waiting for transfers between devices, shards(): from_y = lax.ppermute(to_y, 'band', swap)  15.7 us
    mul x1, other arithmetic, kernel_weights(): return jnp.where(summed > 0.5, profile, 1.0) * (0.25 / float(NG) ** 1.5)  8.2 us
    ppermute x1, waiting for transfers between devices, shards(): p = lax.ppermute(u, 'band', swap)  7.9 us
    ppermute x1, starting transfers between devices, shards(): q = lax.ppermute(u, 'band', there)  6.48 us
  transfers between devices with their start and end apart: 4, of which 3 were waited for; matrix products, arithmetic and copies ran while one was open for 7% of the time, Pallas kernels for 0%

profile of v2, /device:TPU:1, one launch (start us, length us, event | category | flops | bytes accessed | tf_op | source)
XLA Modules:
  0.0 117.0 jit_solution(17832432025855012354)
XLA Ops:
  0.7 0.0 copy-start.1
  0.7 1.2 %copy-done.1 = bf16[1,11,30976]{2,1,0:T(8,128)(2,1)S(1)} copy-done((bf16[1,11,30976]{2,1,0:T(8,128)(2,1)S(1)}, bf16[1,11,30976]{2,1,0:T(8,128)(2,1)}, u32[]{:S(2)}) %copy-start.1) | copy-done | bytes 681496
  1.9 0.0 copy-start.2
  1.9 0.0 copy-start.3
  1.9 0.3 shard_map.91.u_ref
  2.2 6.5 %collective-permute-start.1 = (bf16[11,248,128]{2,1,0:T(8,128)(2,1)S(1)}, bf16[11,248,128]{2,1,0:T(8,128)(2,1)S(1)}, u32[]{:S(2)}, u32[]{:S(2)}) collective-permute-start(bf16[11,248,128]{2,1,0:T(8,128)(2,1)S(1)} %shard_map.91.u_ref), channel_id=1, source_target_pairs={{0,224},{16,48},{32,0},{48,80},{64,32},{80,112},{96,64},{112,144},... | collective-permute-start | bytes 2095112 | tf_op jit(solution)/shard_map/ppermute | solution.py:378
  8.7 0.0 collective-permute-start
  8.7 0.1 broadcast_add_fusion
  8.8 8.2 %fusion.8.w_ref = f32[11,176,256]{2,1,0:T(8,128)S(1)} fusion(f32[256]{0:T(256)} %constant.66, f32[11,176]{1,0:T(8,128)S(1)} %broadcast_add_fusion), kind=kLoop, calls=%fused_computation.10 | loop fusion | flops 4956160 | bytes 1991232 | tf_op jit(solution)/shard_map/mul | solution.py:359
  17.0 7.9 %collective-permute-done.p_ref = bf16[11,248,128]{2,1,0:T(8,128)(2,1)S(1)} collective-permute-done((bf16[11,248,128]{2,1,0:T(8,128)(2,1)S(1)}, bf16[11,248,128]{2,1,0:T(8,128)(2,1)S(1)}, u32[]{:S(2)}, u32[]{:S(2)}) %collective-permute-start) | collective-permute-done | bytes 698400 | tf_op jit(solution)/shard_map/ppermute | solution.py:379
  24.9 0.0 collective-permute-done.1.q_ref
  24.9 0.0 copy-done.2
  24.9 0.0 copy-done.3
  24.9 6.0 %shard_map.92 = s16[16,368,128]{2,1,0:T(8,128)(2,1)S(1)} custom-call(s32[1]{0:T(128)} %bitcast.odd_ref, bf16[11,248,128]{2,1,0:T(8,128)(2,1)S(1)} %shard_map.91.u_ref, bf16[11,248,128]{2,1,0:T(8,128)(2,1)S(1)} %collective-permute-done.p_ref, bf16[11,248,128]{2,1,0:T(8,128)(2,1)S(1)} %collective-permute-done.1.q_ref, bf16[2,400,256]{2,1,0:T(8,128)(2,1)S(1)} %copy-done.2, ...), custom_call_target="tpu_custom_call" | custom-call | flops 1000000000 | bytes 4274180 | tf_op jit(solution)/shard_map/pallas_call | solution.py:336
  30.9 0.0 copy-start.4
  30.9 0.0 copy-start.6
  30.9 30.4 %all_to_all.10.in_ref = s16[16,368,128]{2,1,0:T(8,128)(2,1)S(1)} all-to-all(s16[16,368,128]{2,1,0:T(8,128)(2,1)S(1)} %shard_map.92), channel_id=1, replica_groups=mesh['band'=16,'fft'=16] {'fft'}, dimensions={0} | all-to-all | bytes 3014656 | tf_op jit(solution)/shard_map/all_to_all | solution.py:393
  61.3 0.0 copy-done.4
  61.3 0.0 copy-done.6
  61.3 0.0 copy-start
  61.3 5.3 %shard_map.93 = s16[16,368,128]{2,1,0:T(8,128)(2,1)S(1)} custom-call(s16[16,368,128]{2,1,0:T(8,128)(2,1)S(1)} %all_to_all.10.in_ref, f32[11,176,256]{2,1,0:T(8,128)S(1)} %fusion.8.w_ref, bf16[2,176,256]{2,1,0:T(8,128)(2,1)S(1)} %copy-done.6, bf16[2,256,256]{2,1,0:T(8,128)(2,1)S(1)} %copy-done.4), custom_call_target="tpu_custom_call" | custom-call | flops 1000000000 | bytes 5439488 | tf_op jit(solution)/shard_map/pallas_call | solution.py:336
  66.7 0.0 copy-start.5
  66.7 25.7 %all_to_all.11.in_ref = s16[16,368,128]{2,1,0:T(8,128)(2,1)S(1)} all-to-all(s16[16,368,128]{2,1,0:T(8,128)(2,1)S(1)} %shard_map.93), channel_id=1, replica_groups=mesh['band'=16,'fft'=16] {'fft'}, dimensions={0} | all-to-all | bytes 3014656 | tf_op jit(solution)/shard_map/all_to_all | solution.py:405
  92.4 0.0 copy-done
  92.4 0.0 copy-done.5
  92.4 5.3 %shard_map.94 = (f32[11,248,128]{2,1,0:T(8,128)S(1)}, s16[11,248,128]{2,1,0:T(8,128)(2,1)S(1)}, s16[11,248,128]{2,1,0:T(8,128)(2,1)S(1)}) custom-call(s32[1]{0:T(128)} %bitcast.odd_ref, s16[16,368,128]{2,1,0:T(8,128)(2,1)S(1)} %all_to_all.11.in_ref, bf16[11,248,128]{2,1,0:T(8,128)(2,1)S(1)} %shard_map.91.u_ref, ...), custom_call_target="tpu_custom_call" | custom-call | flops 1000000000 | bytes 10524676 | tf_op jit(solution)/shard_map/pallas_call | solution.py:336
  97.7 0.1 collective-permute-start.2
  97.8 0.1 collective-permute-start.3
  97.9 15.7 %collective-permute-done.2.y_ref = s16[11,248,128]{2,1,0:T(8,128)(2,1)S(1)} collective-permute-done((s16[11,248,128]{2,1,0:T(8,128)(2,1)S(1)}, s16[11,248,128]{2,1,0:T(8,128)(2,1)S(1)}, u32[]{:S(2)}, u32[]{:S(2)}) %collective-permute-start.2) | collective-permute-done | bytes 698400 | tf_op jit(solution)/shard_map/ppermute | solution.py:413
  113.6 1.3 %collective-permute-done.3.z_ref = s16[11,248,128]{2,1,0:T(8,128)(2,1)S(1)} collective-permute-done((s16[11,248,128]{2,1,0:T(8,128)(2,1)S(1)}, s16[11,248,128]{2,1,0:T(8,128)(2,1)S(1)}, u32[]{:S(2)}, u32[]{:S(2)}) %collective-permute-start.3) | collective-permute-done | bytes 698400 | tf_op jit(solution)/shard_map/ppermute | solution.py:412
  114.9 1.9 %shard_map.95 = f32[2662,1,128]{2,1,0:T(1,128)} custom-call(f32[11,248,128]{2,1,0:T(8,128)S(1)} %get-tuple-element.12.own_ref, s16[11,248,128]{2,1,0:T(8,128)(2,1)S(1)} %collective-permute-done.2.y_ref, s16[11,248,128]{2,1,0:T(8,128)(2,1)S(1)} %collective-permute-done.3.z_ref), custom_call_target="tpu_custom_call" | custom-call | bytes 4156416 | tf_op jit(solution)/shard_map/pallas_call | solution.py:336
  (2 shorter events, 0.0 us)
Async XLA Ops:
  0.7 1.2 %copy-start.1 = (bf16[1,11,30976]{2,1,0:T(8,128)(2,1)S(1)}, bf16[1,11,30976]{2,1,0:T(8,128)(2,1)}, u32[]{:S(2)}) copy-start(bf16[1,11,30976]{2,1,0:T(8,128)(2,1)} %param.9) | copy-start | bytes 2044420
  1.9 23.0 %copy-start.2 = (bf16[2,400,256]{2,1,0:T(8,128)(2,1)S(1)}, bf16[2,400,256]{2,1,0:T(8,128)(2,1)}, u32[]{:S(2)}) copy-start(bf16[2,400,256]{2,1,0:T(8,128)(2,1)} %constant.53.clone.zf) | copy-start | bytes 1228804
  1.9 23.0 %copy-start.3 = (bf16[2,256,256]{2,1,0:T(8,128)(2,1)S(1)}, bf16[2,256,256]{2,1,0:T(8,128)(2,1)}, u32[]{:S(2)}) copy-start(bf16[2,256,256]{2,1,0:T(8,128)(2,1)} %constant.54.clone.yf_ref) | copy-start | bytes 786436
  2.2 22.7 %collective-permute-start.1 = (bf16[11,248,128]{2,1,0:T(8,128)(2,1)S(1)}, bf16[11,248,128]{2,1,0:T(8,128)(2,1)S(1)}, u32[]{:S(2)}, u32[]{:S(2)}) collective-permute-start(bf16[11,248,128]{2,1,0:T(8,128)(2,1)S(1)} %shard_map.91.u_ref), channel_id=1, source_target_pairs={{0,224},{16,48},{32,0},{48,80},{64,32},{80,112},{96,64},{112,144},... | collective-permute-start | bytes 2095112 | tf_op jit(solution)/shard_map/ppermute | solution.py:378
  8.7 16.2 %collective-permute-start = (bf16[11,248,128]{2,1,0:T(8,128)(2,1)S(1)}, bf16[11,248,128]{2,1,0:T(8,128)(2,1)S(1)}, u32[]{:S(2)}, u32[]{:S(2)}) collective-permute-start(bf16[11,248,128]{2,1,0:T(8,128)(2,1)S(1)} %shard_map.91.u_ref), channel_id=1, source_target_pairs={{0,16},{16,0},{32,48},{48,32},{64,80},{80,64},{96,112},{112,96},{1... | collective-permute-start | bytes 2095112 | tf_op jit(solution)/shard_map/ppermute | solution.py:379
  30.9 30.4 %copy-start.4 = (bf16[2,256,256]{2,1,0:T(8,128)(2,1)S(1)}, bf16[2,256,256]{2,1,0:T(8,128)(2,1)}, u32[]{:S(2)}) copy-start(bf16[2,256,256]{2,1,0:T(8,128)(2,1)} %constant.56.clone.xb_ref) | copy-start | bytes 786436
  30.9 30.4 %copy-start.6 = (bf16[2,176,256]{2,1,0:T(8,128)(2,1)S(1)}, bf16[2,176,256]{2,1,0:T(8,128)(2,1)}, u32[]{:S(2)}) copy-start(bf16[2,176,256]{2,1,0:T(8,128)(2,1)} %constant.55.clone.xf_ref) | copy-start | bytes 540676
  61.3 31.0 %copy-start = (bf16[2,8,320,384]{3,2,1,0:T(8,128)(2,1)S(1)}, bf16[2,8,320,384]{3,2,1,0:T(8,128)(2,1)}, u32[]{:S(2)}) copy-start(bf16[2,8,320,384]{3,2,1,0:T(8,128)(2,1)} %constant.58.clone.zb) | copy-start | bytes 11796484
  66.7 25.7 %copy-start.5 = (bf16[2,192,256]{2,1,0:T(8,128)(2,1)S(1)}, bf16[2,192,256]{2,1,0:T(8,128)(2,1)}, u32[]{:S(2)}) copy-start(bf16[2,192,256]{2,1,0:T(8,128)(2,1)} %constant.57.clone.yb) | copy-start | bytes 589828
  97.7 15.9 %collective-permute-start.2 = (s16[11,248,128]{2,1,0:T(8,128)(2,1)S(1)}, s16[11,248,128]{2,1,0:T(8,128)(2,1)S(1)}, u32[]{:S(2)}, u32[]{:S(2)}) collective-permute-start(s16[11,248,128]{2,1,0:T(8,128)(2,1)S(1)} %get-tuple-element.13), channel_id=1, source_target_pairs={{0,16},{16,0},{32,48},{48,32},{64,80},{80,64},{96,112},{112,96},{1... | collective-permute-start | bytes 2095112 | tf_op jit(solution)/shard_map/ppermute | solution.py:413
  97.8 17.1 %collective-permute-start.3 = (s16[11,248,128]{2,1,0:T(8,128)(2,1)S(1)}, s16[11,248,128]{2,1,0:T(8,128)(2,1)S(1)}, u32[]{:S(2)}, u32[]{:S(2)}) collective-permute-start(s16[11,248,128]{2,1,0:T(8,128)(2,1)S(1)} %get-tuple-element.14), channel_id=1, source_target_pairs={{224,0},{48,16},{0,32},{80,48},{32,64},{112,80},{64,96},{144,112},... | collective-permute-start | bytes 2095112 | tf_op jit(solution)/shard_map/ppermute | solution.py:412

commit v3 on v2

--- a/solution.py
+++ b/solution.py
@@ -31,6 +31,8 @@
     _first, _offset = divmod(NG * _j, LANES)
     WINDOWS.append((_first, _offset, -(-(_offset + NG) // LANES)))
 
+SHARED = tuple((first, offset) for first, offset, count in WINDOWS if count == 3)
+
 LOW = list(range(8)) + list(range(168, 176))
 KZ_FIRST = list(range(128))
 KZ_REST = list(range(128, 176)) + LOW
@@ -48,24 +50,27 @@
     phase = (index[:, None] * index[None, :] % NG) * (2.0 * np.pi / NG)
     cas = np.cos(phase) + np.sin(phase)
     lanes = np.array(KZ_FIRST + KZ_REST + KZ_REST)
-    z_forward = np.zeros((400, 256))
-    z_forward[112 : 112 + NG] = cas[:, lanes]
-    y_forward = np.zeros((FFT, 16, 256))
-    planes = np.zeros((FFT, 16, 256))
-    for block in range(FFT):
-        own = block * SLAB + np.arange(SLAB)
-        planes[block, :SLAB, :NG] = cas[own]
-        for j in range(8):
-            rows = 8 * np.arange(GROUPS) + j
-            y_forward[block, :SLAB, 24 * j : 24 * j + GROUPS] = cas[own][:, rows]
-    y_forward = y_forward.reshape(256, 256)
-    x_back = planes.reshape(256, 256)
-    x_forward = x_back.T[:NG]
-    y_back = y_forward.T[:192]
-    z_back = np.zeros((8, 320, 384))
-    for j, (_, offset, _) in enumerate(WINDOWS):
-        z_back[j, :128, offset : offset + NG] = cas[KZ_FIRST]
-        z_back[j, 192:256, offset : offset + NG] = cas[KZ_REST]
+    z_forward = np.zeros((8, 256, 256))
+    z_back = np.zeros((8, 256, 256))
+    for j, (_, offset, count) in enumerate(WINDOWS):
+        place = offset + np.arange(NG)
+        if count == 3:
+            place = np.where(place < LANES, place, np.where(place < 256, place, place - 256))
+        z_forward[j, place] = cas[:, lanes]
+        z_back[j, :128, place] = cas[:, KZ_FIRST]
+        z_back[j, 128:192, place] = cas[:, KZ_REST]
+    y_forward = np.zeros((NG, 256))
+    x_back = np.zeros((NG, 256))
+    x_back[:, :NG] = cas
+    y_back = np.zeros((FFT, 16, 192))
+    x_forward = np.zeros((FFT, 16, NG))
+    for j in range(8):
+        rows = 8 * np.arange(GROUPS) + j
+        y_forward[:, 24 * j : 24 * j + GROUPS] = cas[:, rows]
+        y_back[:, :SLAB, 24 * j : 24 * j + GROUPS] = cas[:, rows].reshape(FFT, SLAB, GROUPS)
+    x_forward[:, :SLAB] = cas.reshape(FFT, SLAB, NG)
+    y_back = y_back.reshape(256, 192).T
+    x_forward = x_forward.reshape(256, NG).T
     return {
         "zf": split_table(z_forward),
         "yf": split_table(y_forward),
@@ -105,50 +110,93 @@
     return (jnp.floor(log2 + 0.001) - 14.0).astype(jnp.int32)
 
 
-def numbers(block, first, count, residual_lanes=None):
-    rows = lax.broadcasted_iota(jnp.int32, block.shape, 0)
-    block = jnp.where((rows >= first) & (rows < first + count), block, 0.0)
-    exponent = exponent_of(jnp.max(jnp.abs(block), axis=0, keepdims=True))
-    scaled = block * power_of_two(-exponent)
-    whole = jnp.round(scaled)
+def rounded(value):
+    return (value + 12582912.0) - 12582912.0
+
+
+def largest(*pieces):
+    return functools.reduce(
+        jnp.maximum, [jnp.max(jnp.abs(piece), axis=0, keepdims=True) for piece in pieces]
+    )
+
+
+def part_pieces(blocks, dest, part):
+    window, first = PLACES[part]
+    rows = lax.broadcasted_iota(jnp.int32, (8, LANES), 0)
+    head = blocks[dest, window : window + 8]
+    if first:
+        head = jnp.where(rows >= first, head, 0.0)
+    tail = jnp.where(rows <= first, blocks[dest, window + 120 : window + 128], 0.0)
+    return head, blocks[dest, window + 8 : window + 120], tail
+
+
+def write_blocks(blocks, out_ref, sizes, exponents, residual_lanes=None):
+    for dest in range(FFT):
+        for part in range(PARTS):
+            row = part * FFT + dest
+            sizes[row : row + 1] = largest(*part_pieces(blocks, dest, part))
+    exponent = exponent_of(sizes[...])
+    sizes[...] = power_of_two(-exponent)
     if residual_lanes is not None:
-        whole = jnp.where(residual_lanes, jnp.round((scaled - whole) * 32768.0), whole)
-        exponent = jnp.where(residual_lanes[:1], exponent - 15, exponent)
-    return jnp.where(rows == first + count, exponent, whole.astype(jnp.int32))
-
-
-def write_block(blocks, dest, out_ref, residual_lanes=None):
-    codes = []
-    for part, (window, first) in enumerate(PLACES):
-        lanes = residual_lanes if part == 2 else None
-        codes.append(numbers(blocks[dest, window : window + WINDOW], first, CELLS, lanes))
+        rest = lax.broadcasted_iota(jnp.int32, exponent.shape, 0) >= 2 * FFT
+        exponent = jnp.where(rest & residual_lanes, exponent - 15, exponent)
+    exponents[...] = exponent
     rows = lax.broadcasted_iota(jnp.int32, (8, LANES), 0)
-    pieces = [codes[0][:120]]
-    for part in (1, 2):
-        earlier = codes[part - 1][120:]
-        pieces.append(jnp.where(rows < 2 * part, earlier, codes[part][:8]))
-        pieces.append(codes[part][8:120] if part == 1 else codes[part][8:])
-    out_ref[dest] = jnp.concatenate(pieces, axis=0).astype(jnp.int16)
-
-
-def read_blocks(in_ref, cells):
+    for dest in range(FFT):
+        codes = []
+        for part in range(PARTS):
+            row = part * FFT + dest
+            pieces = []
+            for piece in part_pieces(blocks, dest, part):
+                scaled = piece * sizes[row : row + 1]
+                whole = rounded(scaled)
+                if residual_lanes is not None and part == 2:
+                    rest = rounded((scaled - whole) * 32768.0)
+                    whole = jnp.where(residual_lanes[:1], rest, whole)
+                pieces.append(whole.astype(jnp.int32))
+            first = PLACES[part][1]
+            pieces[2] = jnp.where(rows == first + 1, exponents[row : row + 1], pieces[2])
+            if part:
+                earlier = codes.pop()
+                pieces[0] = jnp.where(rows < first, earlier, pieces[0])
+            codes += pieces
+        out_ref[dest] = jnp.concatenate(codes, axis=0).astype(jnp.int16)
+
+
+def read_blocks(in_ref, cells, sizes):
+    for source in range(FFT):
+        for part, (window, first) in enumerate(PLACES):
+            row = part * FFT + source
+            tiles = in_ref[source, window + 112 : window + 128].astype(F32)
+            sizes[row : row + 1] = tiles[9 + first : 10 + first]
+    sizes[...] = power_of_two(sizes[...].astype(jnp.int32))
     for source in range(FFT):
         block = in_ref[source].astype(jnp.int32)
-        for part, (window, first) in enumerate(PLACES):
-            code = block[window : window + WINDOW]
-            scale = power_of_two(code[first + CELLS : first + CELLS + 1])
-            cells[source, part * WINDOW : (part + 1) * WINDOW] = code.astype(F32) * scale
+        for part, (window, _) in enumerate(PLACES):
+            row = part * FFT + source
+            code = block[window : window + WINDOW].astype(F32)
+            cells[source, part * WINDOW : (part + 1) * WINDOW] = code * sizes[row : row + 1]
         cells[source, PARTS * WINDOW :] = jnp.zeros((56, LANES), F32)
 
 
-def store_cells(blocks, dest, part, line, value):
-    start = part * (CELLS + 1) + line * SLAB
-    size = 16 if line < SLAB - 1 else SLAB
-    blocks[dest, start : start + size] = value[:size]
+def store_field(blocks, lines, field):
+    for place, line in enumerate(lines):
+        for part in range(PARTS):
+            lanes = slice((place * PARTS + part) * LANES, (place * PARTS + part + 1) * LANES)
+            start = part * (CELLS + 1) + line * SLAB
+            for dest in range(FFT):
+                rows = slice(dest * SLAB, (dest + 1) * SLAB)
+                blocks[dest, start : start + SLAB] = field[rows, lanes]
 
 
 def coded(block):
-    return numbers(block, 0, USED)[:SENT].astype(jnp.int16)
+    rows = lax.broadcasted_iota(jnp.int32, (8, LANES), 0)
+    pieces = [block[: SENT - 8], jnp.where(rows < 2, block[SENT - 8 :], 0.0)]
+    exponent = exponent_of(largest(*pieces))
+    scale = power_of_two(-exponent)
+    pieces = [rounded(piece * scale).astype(jnp.int32) for piece in pieces]
+    pieces[1] = jnp.where(rows == 2, exponent, pieces[1])
+    return jnp.concatenate(pieces, axis=0).astype(jnp.int16)
 
 
 def decoded(block):
@@ -166,42 +214,55 @@
 
 
 def density_kernel(
-    odd_ref, u_ref, p_ref, q_ref, zf, yf_ref, out_ref, dens, mixed, blocks, yf, sem
+    odd_ref, u_ref, p_ref, q_ref, zf, yf_ref, out_ref, dens, mixed, blocks, sizes, exponents, yf, sem
 ):
     copy = pltpu.make_async_copy(yf_ref, yf, sem)
     copy.start()
     odd = odd_ref[0] == 1
+    lane = lax.broadcasted_iota(jnp.int32, (2 * SENT, LANES), 1)
+    values = {}
     for step in range(STEPS):
-        lanes = slice(step * LANES, (step + 1) * LANES)
         u, p, q = (ref[step].astype(F32) for ref in (u_ref, p_ref, q_ref))
-        for pair, value in enumerate((jnp.where(odd, u, q) * p, u * q)):
-            value = jnp.concatenate([value, jnp.zeros((ROWS - SENT, LANES), F32)], axis=0)
-            dens[pair, 0, :, lanes], dens[pair, 1, :, lanes] = halves(value)
-    for pair in range(2):
-        for j, (first, offset, count) in enumerate(WINDOWS):
-            lanes = slice(first * LANES, (first + count) * LANES)
-            rows = slice(112 - offset, 112 - offset + count * LANES)
-            mixed[pair, j, :ROWS] = dot3(
-                (dens[pair, 0, :, lanes], dens[pair, 1, :, lanes]), (zf[0, rows], zf[1, rows])
+        values[step] = jnp.concatenate([jnp.where(odd, u, q) * p, u * q], axis=0)
+        tiles = {step: values[step]}
+        for index, (first, offset) in enumerate(SHARED):
+            if step == first + 2:
+                tiles[STEPS + index] = jnp.where(lane >= offset, values[first], values[step])
+        for place, value in tiles.items():
+            lanes = slice(place * LANES, (place + 1) * LANES)
+            dens[0, :, lanes], dens[1, :, lanes] = halves(value)
+    for j, (first, offset, count) in enumerate(WINDOWS):
+        places = (first, first + 1)
+        if count == 3:
+            places = (STEPS + SHARED.index((first, offset)), first + 1)
+        lhs = [
+            jnp.concatenate([dens[h, :, k * LANES : (k + 1) * LANES] for k in places], axis=1)
+            for h in range(2)
+        ]
+        mixed[j] = dot3(lhs, (zf[0, j], zf[1, j]))
+    copy.wait()
+    low_half = lax.broadcasted_iota(jnp.int32, (192, LANES), 1) < 64
+
+    def plane(x):
+        fields = [
+            jnp.concatenate(
+                [mixed[j, start : start + 24] for j in range(8)], axis=0
             )
-    copy.wait()
-    pad = jnp.zeros((64, 256), BF16)
-    low_half = lax.broadcasted_iota(jnp.int32, (ROWS, LANES), 1) < 64
-    for x in range(SLAB):
-        fields = []
-        for pair in range(2):
-            plane = jnp.concatenate(
-                [mixed[pair, j, GROUPS * x : GROUPS * x + 24] for j in range(8)], axis=0
-            )
-            plane = [jnp.concatenate([half, pad], axis=0) for half in halves(plane)]
-            fields.append(dot3((yf[0], yf[1]), plane))
+            for start in (GROUPS * x, SENT + GROUPS * x)
+        ]
         rest = jnp.where(low_half, fields[0][:, LANES:], fields[1][:, LANES:])
-        for part, field in enumerate((fields[0][:, :LANES], fields[1][:, :LANES], rest)):
-            for dest in range(FFT):
-                store_cells(blocks, dest, part, x, field[16 * dest : 16 * dest + 16])
-    residual = (lax.broadcasted_iota(jnp.int32, (WINDOW, LANES), 1) % 64) >= 48
-    for dest in range(FFT):
-        write_block(blocks, dest, out_ref, residual)
+        return jnp.concatenate([fields[0][:, :LANES], fields[1][:, :LANES], rest], axis=1)
+
+    for line in range(0, SLAB, 2):
+        lines = range(line, min(line + 2, SLAB))
+        planes = jnp.concatenate([plane(x) for x in lines], axis=1)
+        pad = jnp.zeros((ROWS - 192, planes.shape[1]), BF16)
+        field = dot3(
+            (yf[0], yf[1]), [jnp.concatenate([half, pad], axis=0) for half in halves(planes)]
+        )
+        store_field(blocks, lines, field)
+    residual = (lax.broadcasted_iota(jnp.int32, sizes.shape, 1) % 64) >= 48
+    write_blocks(blocks, out_ref, sizes, exponents, residual)
 
 
 def gathered(cells, start):
@@ -217,14 +278,16 @@
     return jnp.concatenate(parts, axis=1)
 
 
-def filter_kernel(in_ref, w_ref, xf_ref, xb_ref, out_ref, cells, blocks, xf, xb, sems):
+def filter_kernel(
+    in_ref, w_ref, xf_ref, xb_ref, out_ref, cells, blocks, sizes, exponents, xf, xb, sems
+):
     copies = [
         pltpu.make_async_copy(xf_ref, xf, sems.at[0]),
         pltpu.make_async_copy(xb_ref, xb, sems.at[1]),
     ]
     for copy in copies:
         copy.start()
-    read_blocks(in_ref, cells)
+    read_blocks(in_ref, cells, sizes)
     for copy in copies:
         copy.wait()
     for line in range(0, SLAB, 2):
@@ -238,23 +301,22 @@
         field = dot3(
             (xb[0], xb[1]), [jnp.concatenate([half, pad], axis=0) for half in halves(spectrum)]
         )
-        for place, ky in enumerate(lines):
-            for part in range(PARTS):
-                lanes = slice((place * PARTS + part) * LANES, (place * PARTS + part + 1) * LANES)
-                for dest in range(FFT):
-                    store_cells(blocks, dest, part, ky, field[16 * dest : 16 * dest + 16, lanes])
-    for dest in range(FFT):
-        write_block(blocks, dest, out_ref)
+        store_field(blocks, lines, field)
+    write_blocks(blocks, out_ref, sizes, exponents)
 
 
 def product_kernel(
-    odd_ref, in_ref, u_ref, p_ref, q_ref, yb, zb, own_ref, to_y, to_z, cells, mixed
+    odd_ref, in_ref, u_ref, p_ref, q_ref, yb, zb, own_ref, to_y, to_z, cells, mixed, sizes
 ):
-    read_blocks(in_ref, cells)
-    for x in range(SLAB):
-        plane = dot3((yb[0], yb[1]), halves(gathered(cells, x)))
-        for j in range(8):
-            mixed[j, GROUPS * x : GROUPS * x + 24] = plane[24 * j : 24 * j + 24]
+    read_blocks(in_ref, cells, sizes)
+    for line in range(0, SLAB, 2):
+        lines = range(line, min(line + 2, SLAB))
+        columns = jnp.concatenate([gathered(cells, x) for x in lines], axis=1)
+        planes = dot3((yb[0], yb[1]), halves(columns))
+        for place, x in enumerate(lines):
+            lanes = slice(place * PARTS * LANES, (place + 1) * PARTS * LANES)
+            for j in range(8):
+                mixed[j, GROUPS * x : GROUPS * x + 24] = planes[24 * j : 24 * j + 24, lanes]
     odd = odd_ref[0] == 1
 
     def occupation(ref):
@@ -272,29 +334,26 @@
         to_z[step] = coded(f_u * (v2 * u) + f_send * v1p)
 
     carried = {}
-    used = lax.broadcasted_iota(jnp.int32, (ROWS, PARTS * LANES), 0) < USED
-    for j, (first, _, count) in enumerate(WINDOWS):
-        high, low = halves(jnp.where(used, mixed[j, :ROWS], 0.0))
-        width = slice(0, count * LANES)
-        fields = []
-        for pair in range(2):
-            lhs = [
-                jnp.concatenate(
-                    [half[:, pair * LANES : (pair + 1) * LANES], half[:, 2 * LANES :]], axis=1
-                )
-                for half in (high, low)
-            ]
-            if pair == 0:
-                rhs = [
-                    jnp.concatenate([zb[h, j, 0:128, width], zb[h, j, 192:320, width]], axis=0)
-                    for h in range(2)
-                ]
-            else:
-                rhs = [zb[h, j, 0:256, width] for h in range(2)]
-            fields.append(dot3(lhs, rhs))
+    used = lax.broadcasted_iota(jnp.int32, (SENT, PARTS * LANES), 0) < USED
+    lane = lax.broadcasted_iota(jnp.int32, (SENT, LANES), 1)
+    for j, (first, offset, count) in enumerate(WINDOWS):
+        rows = jnp.where(used, mixed[j, :SENT], 0.0)
+        firsts, seconds, rest = (rows[:, part * LANES : (part + 1) * LANES] for part in range(PARTS))
+        both = jnp.concatenate(
+            [
+                jnp.concatenate([firsts, rest], axis=1),
+                jnp.concatenate([seconds, pltpu.roll(rest, 64, axis=1)], axis=1),
+            ],
+            axis=0,
+        )
+        field = dot3(halves(both), (zb[0, j], zb[1, j]))
+        fields = [field[:SENT], field[SENT:]]
         for k in range(count):
             step = first + k
-            pieces = [field[:SENT, k * LANES : (k + 1) * LANES] for field in fields]
+            pieces = [field[:, k % 2 * LANES : (k % 2 + 1) * LANES] for field in fields]
+            if count == 3 and k != 1:
+                own = lane >= offset if k == 0 else lane < offset
+                pieces = [jnp.where(own, piece, 0.0) for piece in pieces]
             if step in carried:
                 pieces = [a + b for a, b in zip(carried[step], pieces)]
             carried[step] = pieces
@@ -370,6 +429,7 @@
     payload = ((FFT, BLOCK, LANES), jnp.int16)
     cells = pltpu.VMEM((FFT, PARTS * WINDOW + 56, LANES), F32)
     blocks = pltpu.VMEM((FFT, BLOCK, LANES), F32)
+    scales = [pltpu.VMEM((PARTS * FFT, LANES), dtype) for dtype in (F32, jnp.int32)]
 
     u = call(
         compact_kernel, [(layout, BF16)], [SMEM, VMEM],
@@ -382,10 +442,11 @@
     sent = call(
         density_kernel, [payload], [SMEM] + [VMEM] * 4 + [ANY],
         [
-            pltpu.VMEM((2, 2, ROWS, STEPS * LANES), BF16),
-            pltpu.VMEM((2, 8, ROWS + 8, 256), F32),
+            pltpu.VMEM((2, 2 * SENT, (STEPS + 2) * LANES), BF16),
+            pltpu.VMEM((8, 2 * SENT, 256), F32),
             blocks,
-            pltpu.VMEM((2, 256, 256), BF16),
+            *scales,
+            pltpu.VMEM((2, NG, 256), BF16),
             pltpu.SemaphoreType.DMA,
         ],
         (odd, u, p, q, table["zf"], table["yf"]), 10**9, 20,
@@ -396,8 +457,9 @@
         [
             cells,
             blocks,
+            *scales,
             pltpu.VMEM((2, NG, 256), BF16),
-            pltpu.VMEM((2, 256, 256), BF16),
+            pltpu.VMEM((2, NG, 256), BF16),
             pltpu.SemaphoreType.DMA((2,)),
         ],
         (columns, weights, table["xf"], table["xb"]), 10**9, 18,
@@ -406,7 +468,7 @@
     own, to_y, to_z = call(
         product_kernel, [(layout, F32), (layout, jnp.int16), (layout, jnp.int16)],
         [SMEM] + [VMEM] * 6,
-        [cells, pltpu.VMEM((8, ROWS + 8, PARTS * LANES), F32)],
+        [cells, pltpu.VMEM((8, ROWS + 8, PARTS * LANES), F32), scales[0]],
         (odd, slabs, u, p, q, table["yb"], table["zb"]), 10**9, 24,
     )
     from_z = lax.ppermute(to_z, "band", back)

time: 117 us -> 117 us (level)
  Pallas kernels: 18.8 us -> 16.6 us
  local copies, waits for them, and re-layouts: 1.23 us -> 2.82 us
    pallas_call x5, Pallas kernels: 18.8 us -> 16.6 us  [call(): pl.pallas_call(kernel, out_shape=shapes[0] if single else shapes, in_spec...]
    unnamed x14, local copies, waits for them, and re-layouts: 1.23 us -> 2.82 us
where the time goes in v3:
time: 117 us; the launch traced here: 116 us
  blocking collectives  56.1 us (48%)
  waiting for transfers between devices  24.9 us (21%)
  Pallas kernels  16.6 us (14%)
  other arithmetic  8.28 us (7%)
  starting transfers between devices  6.66 us (6%)
  local copies, waits for them, and re-layouts  2.82 us (2%)
    all_to_all x1, blocking collectives, shards(): lax.all_to_all(sent, 'fft', split_axis=0, concat_axis=0, tiled=True)  30.4 us
    all_to_all x1, blocking collectives, shards(): lax.all_to_all(filtered, 'fft', split_axis=0, concat_axis=0, tiled=True)  25.7 us
    pallas_call x5, Pallas kernels, call(): pl.pallas_call(kernel, out_shape=shapes[0] if single else shapes, in_spec...  16.6 us
    ppermute x1, waiting for transfers between devices, shards(): from_y = lax.ppermute(to_y, 'band', swap)  15.7 us
    mul x1, other arithmetic, kernel_weights(): return jnp.where(summed > 0.5, profile, 1.0) * (0.25 / float(NG) ** 1.5)  8.2 us
    ppermute x1, waiting for transfers between devices, shards(): p = lax.ppermute(u, 'band', swap)  7.9 us
    ppermute x1, starting transfers between devices, shards(): q = lax.ppermute(u, 'band', there)  6.48 us
    unnamed x14, local copies, waits for them, and re-layouts  2.82 us
  transfers between devices with their start and end apart: 4, of which 3 were waited for; matrix products, arithmetic and copies ran while one was open for 7% of the time, Pallas kernels for 0%

profile of v3, /device:TPU:1, one launch (start us, length us, event | category | flops | bytes accessed | tf_op | source)
XLA Modules:
  0.0 116.3 jit_solution(571723299339388782)
XLA Ops:
  0.7 0.0 copy-start.2
  0.7 1.2 %copy-done.2 = bf16[1,11,30976]{2,1,0:T(8,128)(2,1)S(1)} copy-done((bf16[1,11,30976]{2,1,0:T(8,128)(2,1)S(1)}, bf16[1,11,30976]{2,1,0:T(8,128)(2,1)}, u32[]{:S(2)}) %copy-start.2) | copy-done | bytes 681496
  1.9 0.0 copy-start.4
  1.9 0.3 shard_map.91.u_ref
  2.2 6.5 %collective-permute-start.1 = (bf16[11,248,128]{2,1,0:T(8,128)(2,1)S(1)}, bf16[11,248,128]{2,1,0:T(8,128)(2,1)S(1)}, u32[]{:S(2)}, u32[]{:S(2)}) collective-permute-start(bf16[11,248,128]{2,1,0:T(8,128)(2,1)S(1)} %shard_map.91.u_ref), channel_id=1, source_target_pairs={{0,224},{16,48},{32,0},{48,80},{64,32},{80,112},{96,64},{112,144},... | collective-permute-start | bytes 2095112 | tf_op jit(solution)/shard_map/ppermute | solution.py:438
  8.7 0.0 collective-permute-start
  8.7 0.1 broadcast_add_fusion
  8.8 8.2 %fusion.8.w_ref = f32[11,176,256]{2,1,0:T(8,128)S(1)} fusion(f32[256]{0:T(256)} %constant.66, f32[11,176]{1,0:T(8,128)S(1)} %broadcast_add_fusion), kind=kLoop, calls=%fused_computation.10 | loop fusion | flops 4956160 | bytes 1991232 | tf_op jit(solution)/shard_map/mul | solution.py:418
  17.0 7.9 %collective-permute-done.p_ref = bf16[11,248,128]{2,1,0:T(8,128)(2,1)S(1)} collective-permute-done((bf16[11,248,128]{2,1,0:T(8,128)(2,1)S(1)}, bf16[11,248,128]{2,1,0:T(8,128)(2,1)S(1)}, u32[]{:S(2)}, u32[]{:S(2)}) %collective-permute-start) | collective-permute-done | bytes 698400 | tf_op jit(solution)/shard_map/ppermute | solution.py:439
  24.9 0.0 collective-permute-done.1.q_ref
  24.9 0.0 copy-done.4
  24.9 0.0 copy-start.1
  24.9 1.6 %copy-done.1 = bf16[2,8,256,256]{3,2,1,0:T(8,128)(2,1)S(1)} copy-done((bf16[2,8,256,256]{3,2,1,0:T(8,128)(2,1)S(1)}, bf16[2,8,256,256]{3,2,1,0:T(8,128)(2,1)}, u32[]{:S(2)}) %copy-start.1) | copy-done | bytes 2097176
  26.5 4.8 %shard_map.92 = s16[16,368,128]{2,1,0:T(8,128)(2,1)S(1)} custom-call(s32[1]{0:T(128)} %bitcast.odd_ref, bf16[11,248,128]{2,1,0:T(8,128)(2,1)S(1)} %shard_map.91.u_ref, bf16[11,248,128]{2,1,0:T(8,128)(2,1)S(1)} %collective-permute-done.p_ref, bf16[11,248,128]{2,1,0:T(8,128)(2,1)S(1)} %collective-permute-done.1.q_ref, bf16[2,8,256,256]{3,2,1,0:T(8,128)(2,1)S(1)} %copy-done.1, ...), custom_call_target="tpu_custom_call" | custom-call | flops 1000000000 | bytes 5879812 | tf_op jit(solution)/shard_map/pallas_call | solution.py:395
  31.2 0.0 copy-start.5
  31.2 0.0 copy-start.6
  31.3 30.4 %all_to_all.10.in_ref = s16[16,368,128]{2,1,0:T(8,128)(2,1)S(1)} all-to-all(s16[16,368,128]{2,1,0:T(8,128)(2,1)S(1)} %shard_map.92), channel_id=1, replica_groups=mesh['band'=16,'fft'=16] {'fft'}, dimensions={0} | all-to-all | bytes 3014656 | tf_op jit(solution)/shard_map/all_to_all | solution.py:454
  61.7 0.0 copy-done.5
  61.7 0.0 copy-done.6
  61.7 4.7 %shard_map.93 = s16[16,368,128]{2,1,0:T(8,128)(2,1)S(1)} custom-call(s16[16,368,128]{2,1,0:T(8,128)(2,1)S(1)} %all_to_all.10.in_ref, f32[11,176,256]{2,1,0:T(8,128)S(1)} %fusion.8.w_ref, bf16[2,176,256]{2,1,0:T(8,128)(2,1)S(1)} %copy-done.6, bf16[2,176,256]{2,1,0:T(8,128)(2,1)S(1)} %copy-done.5), custom_call_target="tpu_custom_call" | custom-call | flops 1000000000 | bytes 5357568 | tf_op jit(solution)/shard_map/pallas_call | solution.py:395
  66.4 0.0 copy-start
  66.4 0.0 copy-start.3
  66.4 25.7 %all_to_all.11.in_ref = s16[16,368,128]{2,1,0:T(8,128)(2,1)S(1)} all-to-all(s16[16,368,128]{2,1,0:T(8,128)(2,1)S(1)} %shard_map.93), channel_id=1, replica_groups=mesh['band'=16,'fft'=16] {'fft'}, dimensions={0} | all-to-all | bytes 3014656 | tf_op jit(solution)/shard_map/all_to_all | solution.py:467
  92.1 0.0 copy-done
  92.1 0.0 copy-done.3
  92.1 5.0 %shard_map.94 = (f32[11,248,128]{2,1,0:T(8,128)S(1)}, s16[11,248,128]{2,1,0:T(8,128)(2,1)S(1)}, s16[11,248,128]{2,1,0:T(8,128)(2,1)S(1)}) custom-call(s32[1]{0:T(128)} %bitcast.odd_ref, s16[16,368,128]{2,1,0:T(8,128)(2,1)S(1)} %all_to_all.11.in_ref, bf16[11,248,128]{2,1,0:T(8,128)(2,1)S(1)} %shard_map.91.u_ref, ...), custom_call_target="tpu_custom_call" | custom-call | flops 1000000000 | bytes 8689668 | tf_op jit(solution)/shard_map/pallas_call | solution.py:395
  97.0 0.1 collective-permute-start.2
  97.1 0.1 collective-permute-start.3
  97.2 15.7 %collective-permute-done.2.y_ref = s16[11,248,128]{2,1,0:T(8,128)(2,1)S(1)} collective-permute-done((s16[11,248,128]{2,1,0:T(8,128)(2,1)S(1)}, s16[11,248,128]{2,1,0:T(8,128)(2,1)S(1)}, u32[]{:S(2)}, u32[]{:S(2)}) %collective-permute-start.2) | collective-permute-done | bytes 698400 | tf_op jit(solution)/shard_map/ppermute | solution.py:475
  113.0 1.3 %collective-permute-done.3.z_ref = s16[11,248,128]{2,1,0:T(8,128)(2,1)S(1)} collective-permute-done((s16[11,248,128]{2,1,0:T(8,128)(2,1)S(1)}, s16[11,248,128]{2,1,0:T(8,128)(2,1)S(1)}, u32[]{:S(2)}, u32[]{:S(2)}) %collective-permute-start.3) | collective-permute-done | bytes 698400 | tf_op jit(solution)/shard_map/ppermute | solution.py:474
  114.3 1.9 %shard_map.95 = f32[2662,1,128]{2,1,0:T(1,128)} custom-call(f32[11,248,128]{2,1,0:T(8,128)S(1)} %get-tuple-element.12.own_ref, s16[11,248,128]{2,1,0:T(8,128)(2,1)S(1)} %collective-permute-done.2.y_ref, s16[11,248,128]{2,1,0:T(8,128)(2,1)S(1)} %collective-permute-done.3.z_ref), custom_call_target="tpu_custom_call" | custom-call | bytes 4156416 | tf_op jit(solution)/shard_map/pallas_call | solution.py:395
  (2 shorter events, 0.0 us)
Async XLA Ops:
  0.7 1.2 %copy-start.2 = (bf16[1,11,30976]{2,1,0:T(8,128)(2,1)S(1)}, bf16[1,11,30976]{2,1,0:T(8,128)(2,1)}, u32[]{:S(2)}) copy-start(bf16[1,11,30976]{2,1,0:T(8,128)(2,1)} %param.9) | copy-start | bytes 2044420
  1.9 23.0 %copy-start.4 = (bf16[2,176,256]{2,1,0:T(8,128)(2,1)S(1)}, bf16[2,176,256]{2,1,0:T(8,128)(2,1)}, u32[]{:S(2)}) copy-start(bf16[2,176,256]{2,1,0:T(8,128)(2,1)} %constant.54.clone.yf_ref) | copy-start | bytes 540676
  2.2 22.7 %collective-permute-start.1 = (bf16[11,248,128]{2,1,0:T(8,128)(2,1)S(1)}, bf16[11,248,128]{2,1,0:T(8,128)(2,1)S(1)}, u32[]{:S(2)}, u32[]{:S(2)}) collective-permute-start(bf16[11,248,128]{2,1,0:T(8,128)(2,1)S(1)} %shard_map.91.u_ref), channel_id=1, source_target_pairs={{0,224},{16,48},{32,0},{48,80},{64,32},{80,112},{96,64},{112,144},... | collective-permute-start | bytes 2095112 | tf_op jit(solution)/shard_map/ppermute | solution.py:438
  8.7 16.2 %collective-permute-start = (bf16[11,248,128]{2,1,0:T(8,128)(2,1)S(1)}, bf16[11,248,128]{2,1,0:T(8,128)(2,1)S(1)}, u32[]{:S(2)}, u32[]{:S(2)}) collective-permute-start(bf16[11,248,128]{2,1,0:T(8,128)(2,1)S(1)} %shard_map.91.u_ref), channel_id=1, source_target_pairs={{0,16},{16,0},{32,48},{48,32},{64,80},{80,64},{96,112},{112,96},{1... | collective-permute-start | bytes 2095112 | tf_op jit(solution)/shard_map/ppermute | solution.py:439
  24.9 1.6 %copy-start.1 = (bf16[2,8,256,256]{3,2,1,0:T(8,128)(2,1)S(1)}, bf16[2,8,256,256]{3,2,1,0:T(8,128)(2,1)}, u32[]{:S(2)}) copy-start(bf16[2,8,256,256]{3,2,1,0:T(8,128)(2,1)} %constant.53.clone.zf) | copy-start | bytes 6291460
  31.2 30.4 %copy-start.5 = (bf16[2,176,256]{2,1,0:T(8,128)(2,1)S(1)}, bf16[2,176,256]{2,1,0:T(8,128)(2,1)}, u32[]{:S(2)}) copy-start(bf16[2,176,256]{2,1,0:T(8,128)(2,1)} %constant.56.clone.xb_ref) | copy-start | bytes 540676
  31.2 30.4 %copy-start.6 = (bf16[2,176,256]{2,1,0:T(8,128)(2,1)S(1)}, bf16[2,176,256]{2,1,0:T(8,128)(2,1)}, u32[]{:S(2)}) copy-start(bf16[2,176,256]{2,1,0:T(8,128)(2,1)} %constant.55.clone.xf_ref) | copy-start | bytes 540676
  66.4 25.7 %copy-start = (bf16[2,8,256,256]{3,2,1,0:T(8,128)(2,1)S(1)}, bf16[2,8,256,256]{3,2,1,0:T(8,128)(2,1)}, u32[]{:S(2)}) copy-start(bf16[2,8,256,256]{3,2,1,0:T(8,128)(2,1)} %constant.58.clone.zb) | copy-start | bytes 6291460
  66.4 25.7 %copy-start.3 = (bf16[2,192,256]{2,1,0:T(8,128)(2,1)S(1)}, bf16[2,192,256]{2,1,0:T(8,128)(2,1)}, u32[]{:S(2)}) copy-start(bf16[2,192,256]{2,1,0:T(8,128)(2,1)} %constant.57.clone.yb) | copy-start | bytes 589828
  97.0 15.9 %collective-permute-start.2 = (s16[11,248,128]{2,1,0:T(8,128)(2,1)S(1)}, s16[11,248,128]{2,1,0:T(8,128)(2,1)S(1)}, u32[]{:S(2)}, u32[]{:S(2)}) collective-permute-start(s16[11,248,128]{2,1,0:T(8,128)(2,1)S(1)} %get-tuple-element.13), channel_id=1, source_target_pairs={{0,16},{16,0},{32,48},{48,32},{64,80},{80,64},{96,112},{112,96},{1... | collective-permute-start | bytes 2095112 | tf_op jit(solution)/shard_map/ppermute | solution.py:475
  97.1 17.1 %collective-permute-start.3 = (s16[11,248,128]{2,1,0:T(8,128)(2,1)S(1)}, s16[11,248,128]{2,1,0:T(8,128)(2,1)S(1)}, u32[]{:S(2)}, u32[]{:S(2)}) collective-permute-start(s16[11,248,128]{2,1,0:T(8,128)(2,1)S(1)} %get-tuple-element.14), channel_id=1, source_target_pairs={{224,0},{48,16},{0,32},{80,48},{32,64},{112,80},{64,96},{144,112},... | collective-permute-start | bytes 2095112 | tf_op jit(solution)/shard_map/ppermute | solution.py:474

commit v4 on v3

--- a/solution.py
+++ b/solution.py
@@ -50,13 +50,15 @@
     phase = (index[:, None] * index[None, :] % NG) * (2.0 * np.pi / NG)
     cas = np.cos(phase) + np.sin(phase)
     lanes = np.array(KZ_FIRST + KZ_REST + KZ_REST)
-    z_forward = np.zeros((8, 256, 256))
+    z_forward = np.zeros((368, 256))
+    z_forward[112 : 112 + NG] = cas[:, lanes]
+    z_shared = np.zeros((len(SHARED), 256, 256))
     z_back = np.zeros((8, 256, 256))
-    for j, (_, offset, count) in enumerate(WINDOWS):
+    for j, (_first, offset, count) in enumerate(WINDOWS):
         place = offset + np.arange(NG)
         if count == 3:
             place = np.where(place < LANES, place, np.where(place < 256, place, place - 256))
-        z_forward[j, place] = cas[:, lanes]
+            z_shared[SHARED.index((_first, offset)), place] = cas[:, lanes]
         z_back[j, :128, place] = cas[:, KZ_FIRST]
         z_back[j, 128:192, place] = cas[:, KZ_REST]
     y_forward = np.zeros((NG, 256))
@@ -73,6 +75,7 @@
     x_forward = x_forward.reshape(256, NG).T
     return {
         "zf": split_table(z_forward),
+        "zs": split_table(z_shared),
         "yf": split_table(y_forward),
         "xf": split_table(x_forward),
         "xb": split_table(x_back),
@@ -214,10 +217,15 @@
 
 
 def density_kernel(
-    odd_ref, u_ref, p_ref, q_ref, zf, yf_ref, out_ref, dens, mixed, blocks, sizes, exponents, yf, sem
+    odd_ref, u_ref, p_ref, q_ref, zf, zs_ref, yf_ref,
+    out_ref, dens, mixed, blocks, sizes, exponents, zs, yf, sems,
 ):
-    copy = pltpu.make_async_copy(yf_ref, yf, sem)
-    copy.start()
+    copies = [
+        pltpu.make_async_copy(zs_ref, zs, sems.at[0]),
+        pltpu.make_async_copy(yf_ref, yf, sems.at[1]),
+    ]
+    for copy in copies:
+        copy.start()
     odd = odd_ref[0] == 1
     lane = lax.broadcasted_iota(jnp.int32, (2 * SENT, LANES), 1)
     values = {}
@@ -232,15 +240,23 @@
             lanes = slice(place * LANES, (place + 1) * LANES)
             dens[0, :, lanes], dens[1, :, lanes] = halves(value)
     for j, (first, offset, count) in enumerate(WINDOWS):
-        places = (first, first + 1)
+        if count == 2:
+            lanes = slice(first * LANES, (first + 2) * LANES)
+            rows = slice(112 - offset, 368 - offset)
+            mixed[j] = dot3((dens[0, :, lanes], dens[1, :, lanes]), (zf[0, rows], zf[1, rows]))
+    for copy in copies:
+        copy.wait()
+    for j, (first, offset, count) in enumerate(WINDOWS):
         if count == 3:
-            places = (STEPS + SHARED.index((first, offset)), first + 1)
-        lhs = [
-            jnp.concatenate([dens[h, :, k * LANES : (k + 1) * LANES] for k in places], axis=1)
-            for h in range(2)
-        ]
-        mixed[j] = dot3(lhs, (zf[0, j], zf[1, j]))
-    copy.wait()
+            index = SHARED.index((first, offset))
+            lhs = [
+                jnp.concatenate(
+                    [dens[h, :, k * LANES : (k + 1) * LANES] for k in (STEPS + index, first + 1)],
+                    axis=1,
+                )
+                for h in range(2)
+            ]
+            mixed[j] = dot3(lhs, (zs[0, index], zs[1, index]))
     low_half = lax.broadcasted_iota(jnp.int32, (192, LANES), 1) < 64
 
     def plane(x):
@@ -440,16 +456,17 @@
     weights = kernel_weights()
     p, weights = lax.optimization_barrier((p, weights))
     sent = call(
-        density_kernel, [payload], [SMEM] + [VMEM] * 4 + [ANY],
+        density_kernel, [payload], [SMEM] + [VMEM] * 4 + [ANY] * 2,
         [
             pltpu.VMEM((2, 2 * SENT, (STEPS + 2) * LANES), BF16),
             pltpu.VMEM((8, 2 * SENT, 256), F32),
             blocks,
             *scales,
+            pltpu.VMEM((2, len(SHARED), 256, 256), BF16),
             pltpu.VMEM((2, NG, 256), BF16),
-            pltpu.SemaphoreType.DMA,
+            pltpu.SemaphoreType.DMA((2,)),
         ],
-        (odd, u, p, q, table["zf"], table["yf"]), 10**9, 20,
+        (odd, u, p, q, table["zf"], table["zs"], table["yf"]), 10**9, 20,
     )
     columns = lax.all_to_all(sent, "fft", split_axis=0, concat_axis=0, tiled=True)
     filtered = call(

time: 117 us -> 115 us (0.983)
  local copies, waits for them, and re-layouts: 2.82 us -> 1.24 us
    unnamed x14 -> x16, local copies, waits for them, and re-layouts: 2.82 us -> 1.24 us
where the time goes in v4:
time: 115 us
  blocking collectives  56.1 us (49%)
  waiting for transfers between devices  24.9 us (22%)
  Pallas kernels  17.1 us (15%)
  other arithmetic  8.28 us (7%)
  starting transfers between devices  6.66 us (6%)
  local copies, waits for them, and re-layouts  1.24 us (1%)
    all_to_all x1, blocking collectives, shards(): lax.all_to_all(sent, 'fft', split_axis=0, concat_axis=0, tiled=True)  30.4 us
    all_to_all x1, blocking collectives, shards(): lax.all_to_all(filtered, 'fft', split_axis=0, concat_axis=0, tiled=True)  25.7 us
    pallas_call x5, Pallas kernels, call(): pl.pallas_call(kernel, out_shape=shapes[0] if single else shapes, in_spec...  17.1 us
    ppermute x1, waiting for transfers between devices, shards(): from_y = lax.ppermute(to_y, 'band', swap)  15.7 us
    mul x1, other arithmetic, kernel_weights(): return jnp.where(summed > 0.5, profile, 1.0) * (0.25 / float(NG) ** 1.5)  8.2 us
    ppermute x1, waiting for transfers between devices, shards(): p = lax.ppermute(u, 'band', swap)  7.9 us
    ppermute x1, starting transfers between devices, shards(): q = lax.ppermute(u, 'band', there)  6.48 us
  transfers between devices with their start and end apart: 4, of which 3 were waited for; matrix products, arithmetic and copies ran while one was open for 7% of the time, Pallas kernels for 0%

profile of v4, /device:TPU:1, one launch (start us, length us, event | category | flops | bytes accessed | tf_op | source)
XLA Modules:
  0.0 115.3 jit_solution(1474882110801396361)
XLA Ops:
  0.7 0.0 copy-start.1
  0.7 1.2 %copy-done.1 = bf16[1,11,30976]{2,1,0:T(8,128)(2,1)S(1)} copy-done((bf16[1,11,30976]{2,1,0:T(8,128)(2,1)S(1)}, bf16[1,11,30976]{2,1,0:T(8,128)(2,1)}, u32[]{:S(2)}) %copy-start.1) | copy-done | bytes 681496
  1.9 0.0 copy-start.2
  1.9 0.0 copy-start.3
  1.9 0.3 shard_map.100.u_ref
  2.2 6.5 %collective-permute-start.1 = (bf16[11,248,128]{2,1,0:T(8,128)(2,1)S(1)}, bf16[11,248,128]{2,1,0:T(8,128)(2,1)S(1)}, u32[]{:S(2)}, u32[]{:S(2)}) collective-permute-start(bf16[11,248,128]{2,1,0:T(8,128)(2,1)S(1)} %shard_map.100.u_ref), channel_id=1, source_target_pairs={{0,224},{16,48},{32,0},{48,80},{64,32},{80,112},{96,64},{112,144},... | collective-permute-start | bytes 2095112 | tf_op jit(solution)/shard_map/ppermute | solution.py:454
  8.7 0.0 collective-permute-start
  8.7 0.1 broadcast_add_fusion
  8.8 8.2 %fusion.8.w_ref = f32[11,176,256]{2,1,0:T(8,128)S(1)} fusion(f32[256]{0:T(256)} %constant.69, f32[11,176]{1,0:T(8,128)S(1)} %broadcast_add_fusion), kind=kLoop, calls=%fused_computation.10 | loop fusion | flops 4956160 | bytes 1991232 | tf_op jit(solution)/shard_map/mul | solution.py:434
  17.0 7.9 %collective-permute-done.p_ref = bf16[11,248,128]{2,1,0:T(8,128)(2,1)S(1)} collective-permute-done((bf16[11,248,128]{2,1,0:T(8,128)(2,1)S(1)}, bf16[11,248,128]{2,1,0:T(8,128)(2,1)S(1)}, u32[]{:S(2)}, u32[]{:S(2)}) %collective-permute-start) | collective-permute-done | bytes 698400 | tf_op jit(solution)/shard_map/ppermute | solution.py:455
  24.9 0.0 collective-permute-done.1.q_ref
  24.9 0.0 copy-done.2
  24.9 0.0 copy-done.3
  24.9 0.0 copy-done.7
  24.9 5.3 %shard_map.101 = s16[16,368,128]{2,1,0:T(8,128)(2,1)S(1)} custom-call(s32[1]{0:T(128)} %bitcast.odd_ref, bf16[11,248,128]{2,1,0:T(8,128)(2,1)S(1)} %shard_map.100.u_ref, bf16[11,248,128]{2,1,0:T(8,128)(2,1)S(1)} %collective-permute-done.p_ref, bf16[11,248,128]{2,1,0:T(8,128)(2,1)S(1)} %collective-permute-done.1.q_ref, bf16[2,368,256]{2,1,0:T(8,128)(2,1)S(1)} %copy-done.3, ...), custom_call_target="tpu_custom_call" | custom-call | flops 1000000000 | bytes 4683780 | tf_op jit(solution)/shard_map/pallas_call | solution.py:411
  30.2 0.0 copy-start.5
  30.2 0.0 copy-start.6
  30.2 30.4 %all_to_all.10.in_ref = s16[16,368,128]{2,1,0:T(8,128)(2,1)S(1)} all-to-all(s16[16,368,128]{2,1,0:T(8,128)(2,1)S(1)} %shard_map.101), channel_id=1, replica_groups=mesh['band'=16,'fft'=16] {'fft'}, dimensions={0} | all-to-all | bytes 3014656 | tf_op jit(solution)/shard_map/all_to_all | solution.py:471
  60.6 0.0 copy-done.5
  60.6 0.0 copy-done.6
  60.6 4.7 %shard_map.102 = s16[16,368,128]{2,1,0:T(8,128)(2,1)S(1)} custom-call(s16[16,368,128]{2,1,0:T(8,128)(2,1)S(1)} %all_to_all.10.in_ref, f32[11,176,256]{2,1,0:T(8,128)S(1)} %fusion.8.w_ref, bf16[2,176,256]{2,1,0:T(8,128)(2,1)S(1)} %copy-done.6, bf16[2,176,256]{2,1,0:T(8,128)(2,1)S(1)} %copy-done.5), custom_call_target="tpu_custom_call" | custom-call | flops 1000000000 | bytes 5357568 | tf_op jit(solution)/shard_map/pallas_call | solution.py:411
  65.3 0.0 copy-start
  65.3 0.0 copy-start.4
  65.4 25.7 %all_to_all.11.in_ref = s16[16,368,128]{2,1,0:T(8,128)(2,1)S(1)} all-to-all(s16[16,368,128]{2,1,0:T(8,128)(2,1)S(1)} %shard_map.102), channel_id=1, replica_groups=mesh['band'=16,'fft'=16] {'fft'}, dimensions={0} | all-to-all | bytes 3014656 | tf_op jit(solution)/shard_map/all_to_all | solution.py:484
  91.0 0.0 copy-done
  91.0 0.0 copy-done.4
  91.0 4.9 %shard_map.103 = (f32[11,248,128]{2,1,0:T(8,128)S(1)}, s16[11,248,128]{2,1,0:T(8,128)(2,1)S(1)}, s16[11,248,128]{2,1,0:T(8,128)(2,1)S(1)}) custom-call(s32[1]{0:T(128)} %bitcast.odd_ref, s16[16,368,128]{2,1,0:T(8,128)(2,1)S(1)} %all_to_all.11.in_ref, bf16[11,248,128]{2,1,0:T(8,128)(2,1)S(1)} %shard_map.100.u_ref, ...), custom_call_target="tpu_custom_call" | custom-call | flops 1000000000 | bytes 8689668 | tf_op jit(solution)/shard_map/pallas_call | solution.py:411
  96.0 0.1 collective-permute-start.2
  96.1 0.1 collective-permute-start.3
  96.2 15.7 %collective-permute-done.2.y_ref = s16[11,248,128]{2,1,0:T(8,128)(2,1)S(1)} collective-permute-done((s16[11,248,128]{2,1,0:T(8,128)(2,1)S(1)}, s16[11,248,128]{2,1,0:T(8,128)(2,1)S(1)}, u32[]{:S(2)}, u32[]{:S(2)}) %collective-permute-start.2) | collective-permute-done | bytes 698400 | tf_op jit(solution)/shard_map/ppermute | solution.py:492
  111.9 1.3 %collective-permute-done.3.z_ref = s16[11,248,128]{2,1,0:T(8,128)(2,1)S(1)} collective-permute-done((s16[11,248,128]{2,1,0:T(8,128)(2,1)S(1)}, s16[11,248,128]{2,1,0:T(8,128)(2,1)S(1)}, u32[]{:S(2)}, u32[]{:S(2)}) %collective-permute-start.3) | collective-permute-done | bytes 698400 | tf_op jit(solution)/shard_map/ppermute | solution.py:491
  113.2 1.9 %shard_map.104 = f32[2662,1,128]{2,1,0:T(1,128)} custom-call(f32[11,248,128]{2,1,0:T(8,128)S(1)} %get-tuple-element.12.own_ref, s16[11,248,128]{2,1,0:T(8,128)(2,1)S(1)} %collective-permute-done.2.y_ref, s16[11,248,128]{2,1,0:T(8,128)(2,1)S(1)} %collective-permute-done.3.z_ref), custom_call_target="tpu_custom_call" | custom-call | bytes 4156416 | tf_op jit(solution)/shard_map/pallas_call | solution.py:411
  (3 shorter events, 0.0 us)
Async XLA Ops:
  0.7 1.2 %copy-start.1 = (bf16[1,11,30976]{2,1,0:T(8,128)(2,1)S(1)}, bf16[1,11,30976]{2,1,0:T(8,128)(2,1)}, u32[]{:S(2)}) copy-start(bf16[1,11,30976]{2,1,0:T(8,128)(2,1)} %param.10) | copy-start | bytes 2044420
  1.9 23.0 %copy-start.2 = (bf16[2,2,256,256]{3,2,1,0:T(8,128)(2,1)S(1)}, bf16[2,2,256,256]{3,2,1,0:T(8,128)(2,1)}, u32[]{:S(2)}) copy-start(bf16[2,2,256,256]{3,2,1,0:T(8,128)(2,1)} %constant.56.clone.zs_ref) | copy-start | bytes 1572868
  1.9 23.0 %copy-start.3 = (bf16[2,368,256]{2,1,0:T(8,128)(2,1)S(1)}, bf16[2,368,256]{2,1,0:T(8,128)(2,1)}, u32[]{:S(2)}) copy-start(bf16[2,368,256]{2,1,0:T(8,128)(2,1)} %constant.55.clone.zf) | copy-start | bytes 1130500
  1.9 23.0 %copy-start.7 = (bf16[2,176,256]{2,1,0:T(8,128)(2,1)S(1)}, bf16[2,176,256]{2,1,0:T(8,128)(2,1)}, u32[]{:S(2)}) copy-start(bf16[2,176,256]{2,1,0:T(8,128)(2,1)} %constant.57.clone.yf_ref) | copy-start | bytes 540676
  2.2 22.7 %collective-permute-start.1 = (bf16[11,248,128]{2,1,0:T(8,128)(2,1)S(1)}, bf16[11,248,128]{2,1,0:T(8,128)(2,1)S(1)}, u32[]{:S(2)}, u32[]{:S(2)}) collective-permute-start(bf16[11,248,128]{2,1,0:T(8,128)(2,1)S(1)} %shard_map.100.u_ref), channel_id=1, source_target_pairs={{0,224},{16,48},{32,0},{48,80},{64,32},{80,112},{96,64},{112,144},... | collective-permute-start | bytes 2095112 | tf_op jit(solution)/shard_map/ppermute | solution.py:454
  8.7 16.2 %collective-permute-start = (bf16[11,248,128]{2,1,0:T(8,128)(2,1)S(1)}, bf16[11,248,128]{2,1,0:T(8,128)(2,1)S(1)}, u32[]{:S(2)}, u32[]{:S(2)}) collective-permute-start(bf16[11,248,128]{2,1,0:T(8,128)(2,1)S(1)} %shard_map.100.u_ref), channel_id=1, source_target_pairs={{0,16},{16,0},{32,48},{48,32},{64,80},{80,64},{96,112},{112,96},{1... | collective-permute-start | bytes 2095112 | tf_op jit(solution)/shard_map/ppermute | solution.py:455
  30.2 30.4 %copy-start.5 = (bf16[2,176,256]{2,1,0:T(8,128)(2,1)S(1)}, bf16[2,176,256]{2,1,0:T(8,128)(2,1)}, u32[]{:S(2)}) copy-start(bf16[2,176,256]{2,1,0:T(8,128)(2,1)} %constant.59.clone.xb_ref) | copy-start | bytes 540676
  30.2 30.4 %copy-start.6 = (bf16[2,176,256]{2,1,0:T(8,128)(2,1)S(1)}, bf16[2,176,256]{2,1,0:T(8,128)(2,1)}, u32[]{:S(2)}) copy-start(bf16[2,176,256]{2,1,0:T(8,128)(2,1)} %constant.58.clone.xf_ref) | copy-start | bytes 540676
  65.3 25.7 %copy-start = (bf16[2,8,256,256]{3,2,1,0:T(8,128)(2,1)S(1)}, bf16[2,8,256,256]{3,2,1,0:T(8,128)(2,1)}, u32[]{:S(2)}) copy-start(bf16[2,8,256,256]{3,2,1,0:T(8,128)(2,1)} %constant.61.clone.zb) | copy-start | bytes 6291460
  65.3 25.7 %copy-start.4 = (bf16[2,192,256]{2,1,0:T(8,128)(2,1)S(1)}, bf16[2,192,256]{2,1,0:T(8,128)(2,1)}, u32[]{:S(2)}) copy-start(bf16[2,192,256]{2,1,0:T(8,128)(2,1)} %constant.60.clone.yb) | copy-start | bytes 589828
  96.0 15.9 %collective-permute-start.2 = (s16[11,248,128]{2,1,0:T(8,128)(2,1)S(1)}, s16[11,248,128]{2,1,0:T(8,128)(2,1)S(1)}, u32[]{:S(2)}, u32[]{:S(2)}) collective-permute-start(s16[11,248,128]{2,1,0:T(8,128)(2,1)S(1)} %get-tuple-element.13), channel_id=1, source_target_pairs={{0,16},{16,0},{32,48},{48,32},{64,80},{80,64},{96,112},{112,96},{1... | collective-permute-start | bytes 2095112 | tf_op jit(solution)/shard_map/ppermute | solution.py:492
  96.1 17.1 %collective-permute-start.3 = (s16[11,248,128]{2,1,0:T(8,128)(2,1)S(1)}, s16[11,248,128]{2,1,0:T(8,128)(2,1)S(1)}, u32[]{:S(2)}, u32[]{:S(2)}) collective-permute-start(s16[11,248,128]{2,1,0:T(8,128)(2,1)S(1)} %get-tuple-element.14), channel_id=1, source_target_pairs={{224,0},{48,16},{0,32},{80,48},{32,64},{112,80},{64,96},{144,112},... | collective-permute-start | bytes 2095112 | tf_op jit(solution)/shard_map/ppermute | solution.py:491

commit v5 on v3

--- a/solution.py
+++ b/solution.py
@@ -50,13 +50,15 @@
     phase = (index[:, None] * index[None, :] % NG) * (2.0 * np.pi / NG)
     cas = np.cos(phase) + np.sin(phase)
     lanes = np.array(KZ_FIRST + KZ_REST + KZ_REST)
-    z_forward = np.zeros((8, 256, 256))
+    z_forward = np.zeros((368, 256))
+    z_forward[112 : 112 + NG] = cas[:, lanes]
+    z_shared = np.zeros((len(SHARED), 256, 256))
     z_back = np.zeros((8, 256, 256))
-    for j, (_, offset, count) in enumerate(WINDOWS):
+    for j, (_first, offset, count) in enumerate(WINDOWS):
         place = offset + np.arange(NG)
         if count == 3:
             place = np.where(place < LANES, place, np.where(place < 256, place, place - 256))
-        z_forward[j, place] = cas[:, lanes]
+            z_shared[SHARED.index((_first, offset)), place] = cas[:, lanes]
         z_back[j, :128, place] = cas[:, KZ_FIRST]
         z_back[j, 128:192, place] = cas[:, KZ_REST]
     y_forward = np.zeros((NG, 256))
@@ -73,6 +75,7 @@
     x_forward = x_forward.reshape(256, NG).T
     return {
         "zf": split_table(z_forward),
+        "zs": split_table(z_shared),
         "yf": split_table(y_forward),
         "xf": split_table(x_forward),
         "xb": split_table(x_back),
@@ -106,7 +109,7 @@
 
 
 def exponent_of(largest):
-    log2 = jnp.log(jnp.maximum(largest, 1e-32)) * F32(1.0 / np.log(2.0))
+    log2 = jnp.log(jnp.maximum(largest, 6.4e-30)) * F32(1.0 / np.log(2.0))
     return (jnp.floor(log2 + 0.001) - 14.0).astype(jnp.int32)
 
 
@@ -214,7 +217,8 @@
 
 
 def density_kernel(
-    odd_ref, u_ref, p_ref, q_ref, zf, yf_ref, out_ref, dens, mixed, blocks, sizes, exponents, yf, sem
+    odd_ref, u_ref, p_ref, q_ref, zf, zs, yf_ref,
+    out_ref, dens, mixed, blocks, sizes, exponents, yf, sem,
 ):
     copy = pltpu.make_async_copy(yf_ref, yf, sem)
     copy.start()
@@ -232,14 +236,19 @@
             lanes = slice(place * LANES, (place + 1) * LANES)
             dens[0, :, lanes], dens[1, :, lanes] = halves(value)
     for j, (first, offset, count) in enumerate(WINDOWS):
-        places = (first, first + 1)
-        if count == 3:
-            places = (STEPS + SHARED.index((first, offset)), first + 1)
+        if count == 2:
+            places = (first, first + 1)
+            rows = slice(112 - offset, 368 - offset)
+            table = (zf[0, rows], zf[1, rows])
+        else:
+            index = SHARED.index((first, offset))
+            places = (STEPS + index, first + 1)
+            table = (zs[0, index], zs[1, index])
         lhs = [
             jnp.concatenate([dens[h, :, k * LANES : (k + 1) * LANES] for k in places], axis=1)
             for h in range(2)
         ]
-        mixed[j] = dot3(lhs, (zf[0, j], zf[1, j]))
+        mixed[j] = dot3(lhs, table)
     copy.wait()
     low_half = lax.broadcasted_iota(jnp.int32, (192, LANES), 1) < 64
 
@@ -440,7 +449,7 @@
     weights = kernel_weights()
     p, weights = lax.optimization_barrier((p, weights))
     sent = call(
-        density_kernel, [payload], [SMEM] + [VMEM] * 4 + [ANY],
+        density_kernel, [payload], [SMEM] + [VMEM] * 5 + [ANY],
         [
             pltpu.VMEM((2, 2 * SENT, (STEPS + 2) * LANES), BF16),
             pltpu.VMEM((8, 2 * SENT, 256), F32),
@@ -449,7 +458,7 @@
             pltpu.VMEM((2, NG, 256), BF16),
             pltpu.SemaphoreType.DMA,
         ],
-        (odd, u, p, q, table["zf"], table["yf"]), 10**9, 20,
+        (odd, u, p, q, table["zf"], table["zs"], table["yf"]), 10**9, 20,
     )
     columns = lax.all_to_all(sent, "fft", split_axis=0, concat_axis=0, tiled=True)
     filtered = call(

time: 117 us -> 115 us (0.983)
  local copies, waits for them, and re-layouts: 2.82 us -> 1.24 us
    unnamed x14 -> x16, local copies, waits for them, and re-layouts: 2.82 us -> 1.24 us
where the time goes in v5:
time: 115 us
  blocking collectives  56.1 us (49%)
  waiting for transfers between devices  24.9 us (22%)
  Pallas kernels  16.9 us (15%)
  other arithmetic  8.28 us (7%)
  starting transfers between devices  6.66 us (6%)
  local copies, waits for them, and re-layouts  1.24 us (1%)
    all_to_all x1, blocking collectives, shards(): lax.all_to_all(sent, 'fft', split_axis=0, concat_axis=0, tiled=True)  30.4 us
    all_to_all x1, blocking collectives, shards(): lax.all_to_all(filtered, 'fft', split_axis=0, concat_axis=0, tiled=True)  25.7 us
    pallas_call x5, Pallas kernels, call(): pl.pallas_call(kernel, out_shape=shapes[0] if single else shapes, in_spec...  16.9 us
    ppermute x1, waiting for transfers between devices, shards(): from_y = lax.ppermute(to_y, 'band', swap)  15.7 us
    mul x1, other arithmetic, kernel_weights(): return jnp.where(summed > 0.5, profile, 1.0) * (0.25 / float(NG) ** 1.5)  8.2 us
    ppermute x1, waiting for transfers between devices, shards(): p = lax.ppermute(u, 'band', swap)  7.9 us
    ppermute x1, starting transfers between devices, shards(): q = lax.ppermute(u, 'band', there)  6.48 us
  transfers between devices with their start and end apart: 4, of which 3 were waited for; matrix products, arithmetic and copies ran while one was open for 7% of the time, Pallas kernels for 0%

profile of v5, /device:TPU:1, one launch (start us, length us, event | category | flops | bytes accessed | tf_op | source)
XLA Modules:
  0.0 115.0 jit_solution(14470858222850748227)
XLA Ops:
  0.7 0.0 copy-start.1
  0.7 1.2 %copy-done.1 = bf16[1,11,30976]{2,1,0:T(8,128)(2,1)S(1)} copy-done((bf16[1,11,30976]{2,1,0:T(8,128)(2,1)S(1)}, bf16[1,11,30976]{2,1,0:T(8,128)(2,1)}, u32[]{:S(2)}) %copy-start.1) | copy-done | bytes 681496
  1.9 0.0 copy-start.2
  1.9 0.0 copy-start.3
  1.9 0.3 shard_map.100.u_ref
  2.2 6.5 %collective-permute-start.1 = (bf16[11,248,128]{2,1,0:T(8,128)(2,1)S(1)}, bf16[11,248,128]{2,1,0:T(8,128)(2,1)S(1)}, u32[]{:S(2)}, u32[]{:S(2)}) collective-permute-start(bf16[11,248,128]{2,1,0:T(8,128)(2,1)S(1)} %shard_map.100.u_ref), channel_id=1, source_target_pairs={{0,224},{16,48},{32,0},{48,80},{64,32},{80,112},{96,64},{112,144},... | collective-permute-start | bytes 2095112 | tf_op jit(solution)/shard_map/ppermute | solution.py:447
  8.7 0.0 collective-permute-start
  8.7 0.1 broadcast_add_fusion
  8.8 8.2 %fusion.8.w_ref = f32[11,176,256]{2,1,0:T(8,128)S(1)} fusion(f32[256]{0:T(256)} %constant.69, f32[11,176]{1,0:T(8,128)S(1)} %broadcast_add_fusion), kind=kLoop, calls=%fused_computation.10 | loop fusion | flops 4956160 | bytes 1991232 | tf_op jit(solution)/shard_map/mul | solution.py:427
  17.0 7.9 %collective-permute-done.p_ref = bf16[11,248,128]{2,1,0:T(8,128)(2,1)S(1)} collective-permute-done((bf16[11,248,128]{2,1,0:T(8,128)(2,1)S(1)}, bf16[11,248,128]{2,1,0:T(8,128)(2,1)S(1)}, u32[]{:S(2)}, u32[]{:S(2)}) %collective-permute-start) | collective-permute-done | bytes 698400 | tf_op jit(solution)/shard_map/ppermute | solution.py:448
  24.9 0.0 collective-permute-done.1.q_ref
  24.9 0.0 copy-done.2
  24.9 0.0 copy-done.3
  24.9 0.0 copy-done.7
  24.9 5.0 %shard_map.101 = s16[16,368,128]{2,1,0:T(8,128)(2,1)S(1)} custom-call(s32[1]{0:T(128)} %bitcast.odd_ref, bf16[11,248,128]{2,1,0:T(8,128)(2,1)S(1)} %shard_map.100.u_ref, bf16[11,248,128]{2,1,0:T(8,128)(2,1)S(1)} %collective-permute-done.p_ref, bf16[11,248,128]{2,1,0:T(8,128)(2,1)S(1)} %collective-permute-done.1.q_ref, bf16[2,368,256]{2,1,0:T(8,128)(2,1)S(1)} %copy-done.3, ...), custom_call_target="tpu_custom_call" | custom-call | flops 1000000000 | bytes 4683780 | tf_op jit(solution)/shard_map/pallas_call | solution.py:404
  29.9 0.0 copy-start.5
  29.9 0.0 copy-start.6
  29.9 30.4 %all_to_all.10.in_ref = s16[16,368,128]{2,1,0:T(8,128)(2,1)S(1)} all-to-all(s16[16,368,128]{2,1,0:T(8,128)(2,1)S(1)} %shard_map.101), channel_id=1, replica_groups=mesh['band'=16,'fft'=16] {'fft'}, dimensions={0} | all-to-all | bytes 3014656 | tf_op jit(solution)/shard_map/all_to_all | solution.py:463
  60.4 0.0 copy-done.5
  60.4 0.0 copy-done.6
  60.4 4.7 %shard_map.102 = s16[16,368,128]{2,1,0:T(8,128)(2,1)S(1)} custom-call(s16[16,368,128]{2,1,0:T(8,128)(2,1)S(1)} %all_to_all.10.in_ref, f32[11,176,256]{2,1,0:T(8,128)S(1)} %fusion.8.w_ref, bf16[2,176,256]{2,1,0:T(8,128)(2,1)S(1)} %copy-done.6, bf16[2,176,256]{2,1,0:T(8,128)(2,1)S(1)} %copy-done.5), custom_call_target="tpu_custom_call" | custom-call | flops 1000000000 | bytes 5357568 | tf_op jit(solution)/shard_map/pallas_call | solution.py:404
  65.1 0.0 copy-start
  65.1 0.0 copy-start.4
  65.1 25.7 %all_to_all.11.in_ref = s16[16,368,128]{2,1,0:T(8,128)(2,1)S(1)} all-to-all(s16[16,368,128]{2,1,0:T(8,128)(2,1)S(1)} %shard_map.102), channel_id=1, replica_groups=mesh['band'=16,'fft'=16] {'fft'}, dimensions={0} | all-to-all | bytes 3014656 | tf_op jit(solution)/shard_map/all_to_all | solution.py:476
  90.8 0.0 copy-done
  90.8 0.0 copy-done.4
  90.8 5.0 %shard_map.103 = (f32[11,248,128]{2,1,0:T(8,128)S(1)}, s16[11,248,128]{2,1,0:T(8,128)(2,1)S(1)}, s16[11,248,128]{2,1,0:T(8,128)(2,1)S(1)}) custom-call(s32[1]{0:T(128)} %bitcast.odd_ref, s16[16,368,128]{2,1,0:T(8,128)(2,1)S(1)} %all_to_all.11.in_ref, bf16[11,248,128]{2,1,0:T(8,128)(2,1)S(1)} %shard_map.100.u_ref, ...), custom_call_target="tpu_custom_call" | custom-call | flops 1000000000 | bytes 8689668 | tf_op jit(solution)/shard_map/pallas_call | solution.py:404
  95.7 0.1 collective-permute-start.2
  95.8 0.1 collective-permute-start.3
  95.9 15.7 %collective-permute-done.2.y_ref = s16[11,248,128]{2,1,0:T(8,128)(2,1)S(1)} collective-permute-done((s16[11,248,128]{2,1,0:T(8,128)(2,1)S(1)}, s16[11,248,128]{2,1,0:T(8,128)(2,1)S(1)}, u32[]{:S(2)}, u32[]{:S(2)}) %collective-permute-start.2) | collective-permute-done | bytes 698400 | tf_op jit(solution)/shard_map/ppermute | solution.py:484
  111.7 1.3 %collective-permute-done.3.z_ref = s16[11,248,128]{2,1,0:T(8,128)(2,1)S(1)} collective-permute-done((s16[11,248,128]{2,1,0:T(8,128)(2,1)S(1)}, s16[11,248,128]{2,1,0:T(8,128)(2,1)S(1)}, u32[]{:S(2)}, u32[]{:S(2)}) %collective-permute-start.3) | collective-permute-done | bytes 698400 | tf_op jit(solution)/shard_map/ppermute | solution.py:483
  113.0 1.9 %shard_map.104 = f32[2662,1,128]{2,1,0:T(1,128)} custom-call(f32[11,248,128]{2,1,0:T(8,128)S(1)} %get-tuple-element.12.own_ref, s16[11,248,128]{2,1,0:T(8,128)(2,1)S(1)} %collective-permute-done.2.y_ref, s16[11,248,128]{2,1,0:T(8,128)(2,1)S(1)} %collective-permute-done.3.z_ref), custom_call_target="tpu_custom_call" | custom-call | bytes 4156416 | tf_op jit(solution)/shard_map/pallas_call | solution.py:404
  (3 shorter events, 0.0 us)
Async XLA Ops:
  0.7 1.2 %copy-start.1 = (bf16[1,11,30976]{2,1,0:T(8,128)(2,1)S(1)}, bf16[1,11,30976]{2,1,0:T(8,128)(2,1)}, u32[]{:S(2)}) copy-start(bf16[1,11,30976]{2,1,0:T(8,128)(2,1)} %param.10) | copy-start | bytes 2044420
  1.9 23.0 %copy-start.2 = (bf16[2,2,256,256]{3,2,1,0:T(8,128)(2,1)S(1)}, bf16[2,2,256,256]{3,2,1,0:T(8,128)(2,1)}, u32[]{:S(2)}) copy-start(bf16[2,2,256,256]{3,2,1,0:T(8,128)(2,1)} %constant.56.clone.zs) | copy-start | bytes 1572868
  1.9 23.0 %copy-start.3 = (bf16[2,368,256]{2,1,0:T(8,128)(2,1)S(1)}, bf16[2,368,256]{2,1,0:T(8,128)(2,1)}, u32[]{:S(2)}) copy-start(bf16[2,368,256]{2,1,0:T(8,128)(2,1)} %constant.55.clone.zf) | copy-start | bytes 1130500
  1.9 23.0 %copy-start.7 = (bf16[2,176,256]{2,1,0:T(8,128)(2,1)S(1)}, bf16[2,176,256]{2,1,0:T(8,128)(2,1)}, u32[]{:S(2)}) copy-start(bf16[2,176,256]{2,1,0:T(8,128)(2,1)} %constant.57.clone.yf_ref) | copy-start | bytes 540676
  2.2 22.7 %collective-permute-start.1 = (bf16[11,248,128]{2,1,0:T(8,128)(2,1)S(1)}, bf16[11,248,128]{2,1,0:T(8,128)(2,1)S(1)}, u32[]{:S(2)}, u32[]{:S(2)}) collective-permute-start(bf16[11,248,128]{2,1,0:T(8,128)(2,1)S(1)} %shard_map.100.u_ref), channel_id=1, source_target_pairs={{0,224},{16,48},{32,0},{48,80},{64,32},{80,112},{96,64},{112,144},... | collective-permute-start | bytes 2095112 | tf_op jit(solution)/shard_map/ppermute | solution.py:447
  8.7 16.2 %collective-permute-start = (bf16[11,248,128]{2,1,0:T(8,128)(2,1)S(1)}, bf16[11,248,128]{2,1,0:T(8,128)(2,1)S(1)}, u32[]{:S(2)}, u32[]{:S(2)}) collective-permute-start(bf16[11,248,128]{2,1,0:T(8,128)(2,1)S(1)} %shard_map.100.u_ref), channel_id=1, source_target_pairs={{0,16},{16,0},{32,48},{48,32},{64,80},{80,64},{96,112},{112,96},{1... | collective-permute-start | bytes 2095112 | tf_op jit(solution)/shard_map/ppermute | solution.py:448
  29.9 30.4 %copy-start.5 = (bf16[2,176,256]{2,1,0:T(8,128)(2,1)S(1)}, bf16[2,176,256]{2,1,0:T(8,128)(2,1)}, u32[]{:S(2)}) copy-start(bf16[2,176,256]{2,1,0:T(8,128)(2,1)} %constant.59.clone.xb_ref) | copy-start | bytes 540676
  29.9 30.4 %copy-start.6 = (bf16[2,176,256]{2,1,0:T(8,128)(2,1)S(1)}, bf16[2,176,256]{2,1,0:T(8,128)(2,1)}, u32[]{:S(2)}) copy-start(bf16[2,176,256]{2,1,0:T(8,128)(2,1)} %constant.58.clone.xf_ref) | copy-start | bytes 540676
  65.1 25.7 %copy-start = (bf16[2,8,256,256]{3,2,1,0:T(8,128)(2,1)S(1)}, bf16[2,8,256,256]{3,2,1,0:T(8,128)(2,1)}, u32[]{:S(2)}) copy-start(bf16[2,8,256,256]{3,2,1,0:T(8,128)(2,1)} %constant.61.clone.zb) | copy-start | bytes 6291460
  65.1 25.7 %copy-start.4 = (bf16[2,192,256]{2,1,0:T(8,128)(2,1)S(1)}, bf16[2,192,256]{2,1,0:T(8,128)(2,1)}, u32[]{:S(2)}) copy-start(bf16[2,192,256]{2,1,0:T(8,128)(2,1)} %constant.60.clone.yb) | copy-start | bytes 589828
  95.7 15.9 %collective-permute-start.2 = (s16[11,248,128]{2,1,0:T(8,128)(2,1)S(1)}, s16[11,248,128]{2,1,0:T(8,128)(2,1)S(1)}, u32[]{:S(2)}, u32[]{:S(2)}) collective-permute-start(s16[11,248,128]{2,1,0:T(8,128)(2,1)S(1)} %get-tuple-element.13), channel_id=1, source_target_pairs={{0,16},{16,0},{32,48},{48,32},{64,80},{80,64},{96,112},{112,96},{1... | collective-permute-start | bytes 2095112 | tf_op jit(solution)/shard_map/ppermute | solution.py:484
  95.8 17.1 %collective-permute-start.3 = (s16[11,248,128]{2,1,0:T(8,128)(2,1)S(1)}, s16[11,248,128]{2,1,0:T(8,128)(2,1)S(1)}, u32[]{:S(2)}, u32[]{:S(2)}) collective-permute-start(s16[11,248,128]{2,1,0:T(8,128)(2,1)S(1)} %get-tuple-element.14), channel_id=1, source_target_pairs={{224,0},{48,16},{0,32},{80,48},{32,64},{112,80},{64,96},{144,112},... | collective-permute-start | bytes 2095112 | tf_op jit(solution)/shard_map/ppermute | solution.py:483

commit v6 on v5

--- a/solution.py
+++ b/solution.py
@@ -138,12 +138,12 @@
         for part in range(PARTS):
             row = part * FFT + dest
             sizes[row : row + 1] = largest(*part_pieces(blocks, dest, part))
-    exponent = exponent_of(sizes[...])
-    sizes[...] = power_of_two(-exponent)
+    exponent = exponent_of(sizes[: PARTS * FFT])
+    sizes[: PARTS * FFT] = power_of_two(-exponent)
     if residual_lanes is not None:
         rest = lax.broadcasted_iota(jnp.int32, exponent.shape, 0) >= 2 * FFT
         exponent = jnp.where(rest & residual_lanes, exponent - 15, exponent)
-    exponents[...] = exponent
+    exponents[: PARTS * FFT] = exponent
     rows = lax.broadcasted_iota(jnp.int32, (8, LANES), 0)
     for dest in range(FFT):
         codes = []
@@ -172,14 +172,14 @@
             row = part * FFT + source
             tiles = in_ref[source, window + 112 : window + 128].astype(F32)
             sizes[row : row + 1] = tiles[9 + first : 10 + first]
-    sizes[...] = power_of_two(sizes[...].astype(jnp.int32))
+    sizes[: PARTS * FFT] = power_of_two(sizes[: PARTS * FFT].astype(jnp.int32))
     for source in range(FFT):
         block = in_ref[source].astype(jnp.int32)
         for part, (window, _) in enumerate(PLACES):
             row = part * FFT + source
             code = block[window : window + WINDOW].astype(F32)
             cells[source, part * WINDOW : (part + 1) * WINDOW] = code * sizes[row : row + 1]
-        cells[source, PARTS * WINDOW :] = jnp.zeros((56, LANES), F32)
+        cells[source, PARTS * WINDOW :] = jnp.zeros((72, LANES), F32)
 
 
 def store_field(blocks, lines, field):
@@ -209,7 +209,7 @@
 
 def compact_kernel(occ_ref, psi_ref, out_ref, scratch):
     for step in range(STEPS):
-        scratch[...] = jnp.full((ROWS, LANES), occ_ref[0], jnp.int32).astype(F32)
+        scratch[:ROWS] = jnp.full((ROWS, LANES), occ_ref[0], jnp.int32).astype(F32)
         for group in range(GROUPS):
             tile = (group * STEPS + step) * LANES
             scratch[pl.ds(group, SLAB, stride=GROUPS), :] = psi_ref[:, tile : tile + LANES].astype(F32)
@@ -248,7 +248,7 @@
             jnp.concatenate([dens[h, :, k * LANES : (k + 1) * LANES] for k in places], axis=1)
             for h in range(2)
         ]
-        mixed[j] = dot3(lhs, table)
+        mixed[j, : 2 * SENT] = dot3(lhs, table)
     copy.wait()
     low_half = lax.broadcasted_iota(jnp.int32, (192, LANES), 1) < 64
 
@@ -270,7 +270,7 @@
             (yf[0], yf[1]), [jnp.concatenate([half, pad], axis=0) for half in halves(planes)]
         )
         store_field(blocks, lines, field)
-    residual = (lax.broadcasted_iota(jnp.int32, sizes.shape, 1) % 64) >= 48
+    residual = (lax.broadcasted_iota(jnp.int32, (PARTS * FFT, LANES), 1) % 64) >= 48
     write_blocks(blocks, out_ref, sizes, exponents, residual)
 
 
@@ -436,13 +436,13 @@
     table = {name: jnp.asarray(value) for name, value in tables().items()}
     layout = (STEPS, SENT, LANES)
     payload = ((FFT, BLOCK, LANES), jnp.int16)
-    cells = pltpu.VMEM((FFT, PARTS * WINDOW + 56, LANES), F32)
-    blocks = pltpu.VMEM((FFT, BLOCK, LANES), F32)
-    scales = [pltpu.VMEM((PARTS * FFT, LANES), dtype) for dtype in (F32, jnp.int32)]
+    cells = pltpu.VMEM((FFT, PARTS * WINDOW + 72, LANES), F32)
+    blocks = pltpu.VMEM((FFT, BLOCK + 16, LANES), F32)
+    scales = [pltpu.VMEM((PARTS * FFT + 16, LANES), dtype) for dtype in (F32, jnp.int32)]
 
     u = call(
         compact_kernel, [(layout, BF16)], [SMEM, VMEM],
-        [pltpu.VMEM((ROWS, LANES), F32)], (band_occ, wavefunctions[0]), 0, 4,
+        [pltpu.VMEM((360, LANES), F32)], (band_occ, wavefunctions[0]), 0, 4,
     )
     q = lax.ppermute(u, "band", there)
     p = lax.ppermute(u, "band", swap)
@@ -452,7 +452,7 @@
         density_kernel, [payload], [SMEM] + [VMEM] * 5 + [ANY],
         [
             pltpu.VMEM((2, 2 * SENT, (STEPS + 2) * LANES), BF16),
-            pltpu.VMEM((8, 2 * SENT, 256), F32),
+            pltpu.VMEM((8, 2 * SENT + 16, 256), F32),
             blocks,
             *scales,
             pltpu.VMEM((2, NG, 256), BF16),
@@ -477,14 +477,14 @@
     own, to_y, to_z = call(
         product_kernel, [(layout, F32), (layout, jnp.int16), (layout, jnp.int16)],
         [SMEM] + [VMEM] * 6,
-        [cells, pltpu.VMEM((8, ROWS + 8, PARTS * LANES), F32), scales[0]],
+        [cells, pltpu.VMEM((8, ROWS + 16, PARTS * LANES), F32), scales[0]],
         (odd, slabs, u, p, q, table["yb"], table["zb"]), 10**9, 24,
     )
     from_z = lax.ppermute(to_z, "band", back)
     from_y = lax.ppermute(to_y, "band", swap)
     result = call(
         sum_kernel, [((SLAB * NG * NG // LANES, 1, LANES), F32)], [VMEM] * 3,
-        [pltpu.VMEM((SLAB * NG * NG // LANES, 1, LANES), F32), pltpu.SemaphoreType.DMA((4,))],
+        [pltpu.VMEM((2736, 1, LANES), F32), pltpu.SemaphoreType.DMA((4,))],
         (own, from_y, from_z), 0, 8, ANY,
     )
     return result.reshape(1, SLAB, NG * NG)

time: 115 us -> 115 us (level)
  no operation moved by 1% of the time
where the time goes in v6:
time: 115 us
  blocking collectives  56.1 us (49%)
  waiting for transfers between devices  24.9 us (22%)
  Pallas kernels  16.8 us (15%)
  other arithmetic  8.28 us (7%)
  starting transfers between devices  6.66 us (6%)
  local copies, waits for them, and re-layouts  1.24 us (1%)
    all_to_all x1, blocking collectives, shards(): lax.all_to_all(sent, 'fft', split_axis=0, concat_axis=0, tiled=True)  30.4 us
    all_to_all x1, blocking collectives, shards(): lax.all_to_all(filtered, 'fft', split_axis=0, concat_axis=0, tiled=True)  25.7 us
    pallas_call x5, Pallas kernels, call(): pl.pallas_call(kernel, out_shape=shapes[0] if single else shapes, in_spec...  16.8 us
    ppermute x1, waiting for transfers between devices, shards(): from_y = lax.ppermute(to_y, 'band', swap)  15.7 us
    mul x1, other arithmetic, kernel_weights(): return jnp.where(summed > 0.5, profile, 1.0) * (0.25 / float(NG) ** 1.5)  8.2 us
    ppermute x1, waiting for transfers between devices, shards(): p = lax.ppermute(u, 'band', swap)  7.9 us
    ppermute x1, starting transfers between devices, shards(): q = lax.ppermute(u, 'band', there)  6.48 us
  transfers between devices with their start and end apart: 4, of which 3 were waited for; matrix products, arithmetic and copies ran while one was open for 7% of the time, Pallas kernels for 0%

profile of v6, /device:TPU:1, one launch (start us, length us, event | category | flops | bytes accessed | tf_op | source)
XLA Modules:
  0.0 115.0 jit_solution(5276450747587442820)
XLA Ops:
  0.7 0.0 copy-start.1
  0.7 1.2 %copy-done.1 = bf16[1,11,30976]{2,1,0:T(8,128)(2,1)S(1)} copy-done((bf16[1,11,30976]{2,1,0:T(8,128)(2,1)S(1)}, bf16[1,11,30976]{2,1,0:T(8,128)(2,1)}, u32[]{:S(2)}) %copy-start.1) | copy-done | bytes 681496
  1.9 0.0 copy-start.2
  1.9 0.0 copy-start.3
  1.9 0.3 shard_map.100.u_ref
  2.2 6.5 %collective-permute-start.1 = (bf16[11,248,128]{2,1,0:T(8,128)(2,1)S(1)}, bf16[11,248,128]{2,1,0:T(8,128)(2,1)S(1)}, u32[]{:S(2)}, u32[]{:S(2)}) collective-permute-start(bf16[11,248,128]{2,1,0:T(8,128)(2,1)S(1)} %shard_map.100.u_ref), channel_id=1, source_target_pairs={{0,224},{16,48},{32,0},{48,80},{64,32},{80,112},{96,64},{112,144},... | collective-permute-start | bytes 2095112 | tf_op jit(solution)/shard_map/ppermute | solution.py:447
  8.7 0.0 collective-permute-start
  8.7 0.1 broadcast_add_fusion
  8.8 8.2 %fusion.8.w_ref = f32[11,176,256]{2,1,0:T(8,128)S(1)} fusion(f32[256]{0:T(256)} %constant.69, f32[11,176]{1,0:T(8,128)S(1)} %broadcast_add_fusion), kind=kLoop, calls=%fused_computation.10 | loop fusion | flops 4956160 | bytes 1991232 | tf_op jit(solution)/shard_map/mul | solution.py:427
  17.0 7.9 %collective-permute-done.p_ref = bf16[11,248,128]{2,1,0:T(8,128)(2,1)S(1)} collective-permute-done((bf16[11,248,128]{2,1,0:T(8,128)(2,1)S(1)}, bf16[11,248,128]{2,1,0:T(8,128)(2,1)S(1)}, u32[]{:S(2)}, u32[]{:S(2)}) %collective-permute-start) | collective-permute-done | bytes 698400 | tf_op jit(solution)/shard_map/ppermute | solution.py:448
  24.9 0.0 collective-permute-done.1.q_ref
  24.9 0.0 copy-done.2
  24.9 0.0 copy-done.3
  24.9 0.0 copy-done.7
  24.9 5.0 %shard_map.101 = s16[16,368,128]{2,1,0:T(8,128)(2,1)S(1)} custom-call(s32[1]{0:T(128)} %bitcast.odd_ref, bf16[11,248,128]{2,1,0:T(8,128)(2,1)S(1)} %shard_map.100.u_ref, bf16[11,248,128]{2,1,0:T(8,128)(2,1)S(1)} %collective-permute-done.p_ref, bf16[11,248,128]{2,1,0:T(8,128)(2,1)S(1)} %collective-permute-done.1.q_ref, bf16[2,368,256]{2,1,0:T(8,128)(2,1)S(1)} %copy-done.3, ...), custom_call_target="tpu_custom_call" | custom-call | flops 1000000000 | bytes 4683780 | tf_op jit(solution)/shard_map/pallas_call | solution.py:404
  29.9 0.0 copy-start.5
  29.9 0.0 copy-start.6
  29.9 30.4 %all_to_all.10.in_ref = s16[16,368,128]{2,1,0:T(8,128)(2,1)S(1)} all-to-all(s16[16,368,128]{2,1,0:T(8,128)(2,1)S(1)} %shard_map.101), channel_id=1, replica_groups=mesh['band'=16,'fft'=16] {'fft'}, dimensions={0} | all-to-all | bytes 3014656 | tf_op jit(solution)/shard_map/all_to_all | solution.py:463
  60.4 0.0 copy-done.5
  60.4 0.0 copy-done.6
  60.4 4.7 %shard_map.102 = s16[16,368,128]{2,1,0:T(8,128)(2,1)S(1)} custom-call(s16[16,368,128]{2,1,0:T(8,128)(2,1)S(1)} %all_to_all.10.in_ref, f32[11,176,256]{2,1,0:T(8,128)S(1)} %fusion.8.w_ref, bf16[2,176,256]{2,1,0:T(8,128)(2,1)S(1)} %copy-done.6, bf16[2,176,256]{2,1,0:T(8,128)(2,1)S(1)} %copy-done.5), custom_call_target="tpu_custom_call" | custom-call | flops 1000000000 | bytes 5357568 | tf_op jit(solution)/shard_map/pallas_call | solution.py:404
  65.1 0.0 copy-start
  65.1 0.0 copy-start.4
  65.1 25.7 %all_to_all.11.in_ref = s16[16,368,128]{2,1,0:T(8,128)(2,1)S(1)} all-to-all(s16[16,368,128]{2,1,0:T(8,128)(2,1)S(1)} %shard_map.102), channel_id=1, replica_groups=mesh['band'=16,'fft'=16] {'fft'}, dimensions={0} | all-to-all | bytes 3014656 | tf_op jit(solution)/shard_map/all_to_all | solution.py:476
  90.8 0.0 copy-done
  90.8 0.0 copy-done.4
  90.8 4.9 %shard_map.103 = (f32[11,248,128]{2,1,0:T(8,128)S(1)}, s16[11,248,128]{2,1,0:T(8,128)(2,1)S(1)}, s16[11,248,128]{2,1,0:T(8,128)(2,1)S(1)}) custom-call(s32[1]{0:T(128)} %bitcast.odd_ref, s16[16,368,128]{2,1,0:T(8,128)(2,1)S(1)} %all_to_all.11.in_ref, bf16[11,248,128]{2,1,0:T(8,128)(2,1)S(1)} %shard_map.100.u_ref, ...), custom_call_target="tpu_custom_call" | custom-call | flops 1000000000 | bytes 8689668 | tf_op jit(solution)/shard_map/pallas_call | solution.py:404
  95.7 0.1 collective-permute-start.2
  95.8 0.1 collective-permute-start.3
  95.9 15.7 %collective-permute-done.2.y_ref = s16[11,248,128]{2,1,0:T(8,128)(2,1)S(1)} collective-permute-done((s16[11,248,128]{2,1,0:T(8,128)(2,1)S(1)}, s16[11,248,128]{2,1,0:T(8,128)(2,1)S(1)}, u32[]{:S(2)}, u32[]{:S(2)}) %collective-permute-start.2) | collective-permute-done | bytes 698400 | tf_op jit(solution)/shard_map/ppermute | solution.py:484
  111.6 1.3 %collective-permute-done.3.z_ref = s16[11,248,128]{2,1,0:T(8,128)(2,1)S(1)} collective-permute-done((s16[11,248,128]{2,1,0:T(8,128)(2,1)S(1)}, s16[11,248,128]{2,1,0:T(8,128)(2,1)S(1)}, u32[]{:S(2)}, u32[]{:S(2)}) %collective-permute-start.3) | collective-permute-done | bytes 698400 | tf_op jit(solution)/shard_map/ppermute | solution.py:483
  112.9 1.9 %shard_map.104 = f32[2662,1,128]{2,1,0:T(1,128)} custom-call(f32[11,248,128]{2,1,0:T(8,128)S(1)} %get-tuple-element.12.own_ref, s16[11,248,128]{2,1,0:T(8,128)(2,1)S(1)} %collective-permute-done.2.y_ref, s16[11,248,128]{2,1,0:T(8,128)(2,1)S(1)} %collective-permute-done.3.z_ref), custom_call_target="tpu_custom_call" | custom-call | bytes 4156416 | tf_op jit(solution)/shard_map/pallas_call | solution.py:404
  (3 shorter events, 0.0 us)
Async XLA Ops:
  0.7 1.2 %copy-start.1 = (bf16[1,11,30976]{2,1,0:T(8,128)(2,1)S(1)}, bf16[1,11,30976]{2,1,0:T(8,128)(2,1)}, u32[]{:S(2)}) copy-start(bf16[1,11,30976]{2,1,0:T(8,128)(2,1)} %param.10) | copy-start | bytes 2044420
  1.9 23.0 %copy-start.2 = (bf16[2,2,256,256]{3,2,1,0:T(8,128)(2,1)S(1)}, bf16[2,2,256,256]{3,2,1,0:T(8,128)(2,1)}, u32[]{:S(2)}) copy-start(bf16[2,2,256,256]{3,2,1,0:T(8,128)(2,1)} %constant.56.clone.zs) | copy-start | bytes 1572868
  1.9 23.0 %copy-start.3 = (bf16[2,368,256]{2,1,0:T(8,128)(2,1)S(1)}, bf16[2,368,256]{2,1,0:T(8,128)(2,1)}, u32[]{:S(2)}) copy-start(bf16[2,368,256]{2,1,0:T(8,128)(2,1)} %constant.55.clone.zf) | copy-start | bytes 1130500
  1.9 23.0 %copy-start.7 = (bf16[2,176,256]{2,1,0:T(8,128)(2,1)S(1)}, bf16[2,176,256]{2,1,0:T(8,128)(2,1)}, u32[]{:S(2)}) copy-start(bf16[2,176,256]{2,1,0:T(8,128)(2,1)} %constant.57.clone.yf_ref) | copy-start | bytes 540676
  2.2 22.7 %collective-permute-start.1 = (bf16[11,248,128]{2,1,0:T(8,128)(2,1)S(1)}, bf16[11,248,128]{2,1,0:T(8,128)(2,1)S(1)}, u32[]{:S(2)}, u32[]{:S(2)}) collective-permute-start(bf16[11,248,128]{2,1,0:T(8,128)(2,1)S(1)} %shard_map.100.u_ref), channel_id=1, source_target_pairs={{0,224},{16,48},{32,0},{48,80},{64,32},{80,112},{96,64},{112,144},... | collective-permute-start | bytes 2095112 | tf_op jit(solution)/shard_map/ppermute | solution.py:447
  8.7 16.2 %collective-permute-start = (bf16[11,248,128]{2,1,0:T(8,128)(2,1)S(1)}, bf16[11,248,128]{2,1,0:T(8,128)(2,1)S(1)}, u32[]{:S(2)}, u32[]{:S(2)}) collective-permute-start(bf16[11,248,128]{2,1,0:T(8,128)(2,1)S(1)} %shard_map.100.u_ref), channel_id=1, source_target_pairs={{0,16},{16,0},{32,48},{48,32},{64,80},{80,64},{96,112},{112,96},{1... | collective-permute-start | bytes 2095112 | tf_op jit(solution)/shard_map/ppermute | solution.py:448
  29.9 30.4 %copy-start.5 = (bf16[2,176,256]{2,1,0:T(8,128)(2,1)S(1)}, bf16[2,176,256]{2,1,0:T(8,128)(2,1)}, u32[]{:S(2)}) copy-start(bf16[2,176,256]{2,1,0:T(8,128)(2,1)} %constant.59.clone.xb_ref) | copy-start | bytes 540676
  29.9 30.4 %copy-start.6 = (bf16[2,176,256]{2,1,0:T(8,128)(2,1)S(1)}, bf16[2,176,256]{2,1,0:T(8,128)(2,1)}, u32[]{:S(2)}) copy-start(bf16[2,176,256]{2,1,0:T(8,128)(2,1)} %constant.58.clone.xf_ref) | copy-start | bytes 540676
  65.1 25.7 %copy-start = (bf16[2,8,256,256]{3,2,1,0:T(8,128)(2,1)S(1)}, bf16[2,8,256,256]{3,2,1,0:T(8,128)(2,1)}, u32[]{:S(2)}) copy-start(bf16[2,8,256,256]{3,2,1,0:T(8,128)(2,1)} %constant.61.clone.zb) | copy-start | bytes 6291460
  65.1 25.7 %copy-start.4 = (bf16[2,192,256]{2,1,0:T(8,128)(2,1)S(1)}, bf16[2,192,256]{2,1,0:T(8,128)(2,1)}, u32[]{:S(2)}) copy-start(bf16[2,192,256]{2,1,0:T(8,128)(2,1)} %constant.60.clone.yb) | copy-start | bytes 589828
  95.7 15.9 %collective-permute-start.2 = (s16[11,248,128]{2,1,0:T(8,128)(2,1)S(1)}, s16[11,248,128]{2,1,0:T(8,128)(2,1)S(1)}, u32[]{:S(2)}, u32[]{:S(2)}) collective-permute-start(s16[11,248,128]{2,1,0:T(8,128)(2,1)S(1)} %get-tuple-element.13), channel_id=1, source_target_pairs={{0,16},{16,0},{32,48},{48,32},{64,80},{80,64},{96,112},{112,96},{1... | collective-permute-start | bytes 2095112 | tf_op jit(solution)/shard_map/ppermute | solution.py:484
  95.8 17.1 %collective-permute-start.3 = (s16[11,248,128]{2,1,0:T(8,128)(2,1)S(1)}, s16[11,248,128]{2,1,0:T(8,128)(2,1)S(1)}, u32[]{:S(2)}, u32[]{:S(2)}) collective-permute-start(s16[11,248,128]{2,1,0:T(8,128)(2,1)S(1)} %get-tuple-element.14), channel_id=1, source_target_pairs={{224,0},{48,16},{0,32},{80,48},{32,64},{112,80},{64,96},{144,112},... | collective-permute-start | bytes 2095112 | tf_op jit(solution)/shard_map/ppermute | solution.py:483
